TPU v7x, 512 devices: a whole 4x4x16 slice. The times are simulated.
512 devices in a mesh: pipe: 2 (over core), expert: 64 (over y, z), dp: 4 (over x).
Axes of the slice: x: 4, y: 4, z: 16, core: 2. Of those that a mesh axis runs over, the one named last changes fastest.
Arguments:
- tokens: bfloat16 [2, 2048, 3584], P('pipe', ('expert', 'dp')), may hold values from -6 to 6
- grad_out: bfloat16 [2, 2048, 3584], P('pipe', ('expert', 'dp')), may hold values from -1.5 to 1.5
- routes: int32 [2, 2048, 4], P('pipe', ('expert', 'dp')), may hold values from 0 to 7, all different within a row; in each aligned block of 8 rows (0 to 7, 8 to 15, ..., all dimensions but the last counted through in order) at most 6 rows name the same one
- combine: bfloat16 [2, 2048, 4], P('pipe', ('expert', 'dp')), may hold values from 0.25 to 2.5
- w_gate: bfloat16 [2, 3584, 8192], P('pipe', 'dp', 'expert'), may hold values from -0.09375 to 0.09375
- w_up: bfloat16 [2, 3584, 8192], P('pipe', 'dp', 'expert'), may hold values from -0.09375 to 0.09375
- w_down: bfloat16 [2, 3584, 8192], P('pipe', 'dp', 'expert'), may hold values from -0.1875 to 0.1875
Outputs:
- passed: bfloat16 [2, 2048, 3584], P('pipe', ('expert', 'dp'))
- grad_combine: float32 [2, 2048, 4], P('pipe', ('expert', 'dp'))
- grad_gate: float32 [2, 3584, 8192], P('pipe', 'dp', 'expert')
- grad_up: float32 [2, 3584, 8192], P('pipe', 'dp', 'expert')
- grad_down: float32 [2, 3584, 8192], P('pipe', 'dp', 'expert')
Inputs may be any that keep to these rules, and one draw needn't show every extreme that they name: `routes`: each token names 4 different experts; among the 8 tokens of one device no expert is named more than 6 times, and in some device's tokens an expert is named exactly 6 times.
All inputs are finite; a program needn't handle non-finite values.
Results may differ from a plain program's by a relative error of at most 0.012.
Values may be sent and summed in bfloat16 or wider, within the bound.
No kernel may reach another device: no remote copies, remote signals or barrier semaphores. Data moves between devices by JAX's collectives and lax.ppermute only.
A program may use at most 128 MiB of HBM per device.

v0:
```python
import jax
import jax.numpy as jnp
from jax import lax
from jax.sharding import PartitionSpec as P

contract_last = (((1,), (1,)), ((), ()))
contract_first = (((0,), (0,)), ((), ()))


def from_behind(block, axis, distance):
    devices = range(lax.axis_size(axis))
    route = [((i - distance) % len(devices), i) for i in devices]
    return lax.ppermute(block, axis, route)


def activate(gate_pre, up_pre):
    sigmoid_gate = jax.nn.sigmoid(gate_pre)
    activated = gate_pre * sigmoid_gate
    hidden = (activated * up_pre).astype(jnp.bfloat16)
    return (sigmoid_gate, activated, hidden)


def backprop_hidden(hidden_grad, gate_pre, up_pre, sigmoid_gate, activated):
    gate_grad = (
        hidden_grad * up_pre * sigmoid_gate * (1.0 + gate_pre * (1.0 - sigmoid_gate))
    ).astype(jnp.bfloat16)
    up_grad = (hidden_grad * activated).astype(jnp.bfloat16)
    return (gate_grad, up_grad)


def body(tokens, grad_out, routes, combine, w_gate, w_up, w_down):
    model_width = tokens.shape[2]
    tok_count = tokens.shape[1]
    top_count = routes.shape[2]
    hidden_dev = w_gate.shape[2]
    devices = lax.axis_size("expert")
    slices = min(8, devices // 2)
    expert_count = devices // slices
    capacity = min(tok_count, max(2, 3 * tok_count * top_count // (2 * expert_count)))
    slot_count = expert_count * capacity
    flat_routes = routes[0].reshape(-1)
    onehot = (flat_routes[:, None] == jnp.arange(expert_count, dtype=jnp.int32)[None, :]).astype(
        jnp.int32
    )
    earlier = jnp.cumsum(onehot, axis=0) - onehot
    position = jnp.sum(earlier * onehot, axis=1)
    slot_of = flat_routes * capacity + position
    placed = slot_of[None, :] == jnp.arange(slot_count, dtype=jnp.int32)[:, None]
    placed_float = placed.astype(jnp.float32)
    owner_mask = jnp.any(placed.reshape(slot_count, tok_count, top_count), axis=2)
    owner_half = owner_mask.astype(jnp.bfloat16)
    slot_inputs = jnp.dot(owner_half, tokens[0], preferred_element_type=jnp.float32).astype(
        jnp.bfloat16
    )
    slot_cotangent = jnp.dot(owner_half, grad_out[0], preferred_element_type=jnp.float32).astype(
        jnp.bfloat16
    )
    slot_weight = jnp.dot(
        placed.astype(jnp.bfloat16), combine[0].reshape(-1), preferred_element_type=jnp.float32
    ).astype(jnp.bfloat16)

    def replicate_slots(array):
        tail_shape = array.shape[1:]
        shaped = array.reshape((expert_count, 1, capacity) + tail_shape)
        spread = jnp.broadcast_to(shaped, (expert_count, slices, capacity) + tail_shape)
        return spread.reshape((devices, capacity) + tail_shape)

    got_inputs, got_cotangent, got_weight = (
        lax.all_to_all(
            replicate_slots(slot_inputs), "expert", split_axis=0, concat_axis=0, tiled=True
        ),
        lax.all_to_all(
            replicate_slots(slot_cotangent), "expert", split_axis=0, concat_axis=0, tiled=True
        ),
        lax.all_to_all(
            replicate_slots(slot_weight), "expert", split_axis=0, concat_axis=0, tiled=True
        ),
    )
    row_count = devices * capacity
    row_inputs = got_inputs.reshape(row_count, model_width)
    row_cotangent = got_cotangent.reshape(row_count, model_width)
    row_weight = got_weight.reshape(row_count).astype(jnp.float32)
    out_grad = (row_weight[:, None] * row_cotangent.astype(jnp.float32)).astype(jnp.bfloat16)
    full_gate, full_up, full_down = (
        lax.all_gather(w_gate, "dp", axis=1, tiled=True),
        lax.all_gather(w_up, "dp", axis=1, tiled=True),
        lax.all_gather(w_down, "dp", axis=1, tiled=True),
    )
    gate_mat = full_gate[0]
    up_mat = full_up[0]
    down_mat = full_down[0]
    gate_pre = jnp.dot(row_inputs, gate_mat, preferred_element_type=jnp.float32)
    up_pre = jnp.dot(row_inputs, up_mat, preferred_element_type=jnp.float32)
    sigmoid_gate, activated, hidden = activate(gate_pre, up_pre)
    expert_out = lax.dot_general(
        hidden, down_mat, contract_last, preferred_element_type=jnp.float32
    )
    hidden_grad = jnp.dot(out_grad, down_mat, preferred_element_type=jnp.float32)
    gate_grad, up_grad = backprop_hidden(hidden_grad, gate_pre, up_pre, sigmoid_gate, activated)
    input_rows = lax.dot_general(
        gate_grad, gate_mat, contract_last, preferred_element_type=jnp.float32
    )
    input_rows = input_rows + lax.dot_general(
        up_grad, up_mat, contract_last, preferred_element_type=jnp.float32
    )
    route_score = jnp.sum(expert_out * row_cotangent.astype(jnp.float32), axis=1)
    back_rows, back_score = (
        lax.all_to_all(
            input_rows.reshape(devices, capacity, model_width).astype(jnp.bfloat16),
            "expert",
            split_axis=0,
            concat_axis=0,
            tiled=True,
        ).astype(jnp.float32),
        lax.all_to_all(
            route_score.reshape(devices, capacity).astype(jnp.bfloat16),
            "expert",
            split_axis=0,
            concat_axis=0,
            tiled=True,
        ).astype(jnp.float32),
    )
    slot_grad = jnp.sum(back_rows.reshape(expert_count, slices, capacity, model_width), axis=1)
    slot_grad = slot_grad.reshape(slot_count, model_width)
    slot_score = jnp.sum(back_score.reshape(expert_count, slices, capacity), axis=1).reshape(
        slot_count
    )
    token_grad = lax.dot_general(
        owner_mask.astype(jnp.float32),
        slot_grad,
        contract_first,
        precision=lax.Precision.HIGHEST,
        preferred_element_type=jnp.float32,
    )
    route_grad = lax.dot_general(
        placed_float,
        slot_score,
        contract_first,
        precision=lax.Precision.HIGHEST,
        preferred_element_type=jnp.float32,
    )
    passed = from_behind(token_grad.astype(jnp.bfloat16)[None], "pipe", -1)
    shares = lax.psum_scatter(
        jnp.concatenate(
            [
                lax.dot_general(
                    row_inputs, gate_grad, contract_first, preferred_element_type=jnp.float32
                ),
                lax.dot_general(
                    row_inputs, up_grad, contract_first, preferred_element_type=jnp.float32
                ),
                lax.dot_general(
                    out_grad, hidden, contract_first, preferred_element_type=jnp.float32
                ),
            ],
            axis=1,
        ).astype(jnp.bfloat16),
        "dp",
        scatter_dimension=0,
        tiled=True,
    ).astype(jnp.float32)
    grad_gate = shares[:, :hidden_dev][None]
    grad_up = shares[:, hidden_dev : 2 * hidden_dev][None]
    grad_down = shares[:, 2 * hidden_dev :][None]
    return (passed, route_grad.reshape(1, tok_count, top_count), grad_gate, grad_up, grad_down)


def solution(mesh):
    in_specs = (
        P("pipe", ("expert", "dp"), None),
        P("pipe", ("expert", "dp"), None),
        P("pipe", ("expert", "dp"), None),
        P("pipe", ("expert", "dp"), None),
        P("pipe", "dp", "expert"),
        P("pipe", "dp", "expert"),
        P("pipe", "dp", "expert"),
    )
    out_specs = (
        P("pipe", ("expert", "dp"), None),
        P("pipe", ("expert", "dp"), None),
        P("pipe", "dp", "expert"),
        P("pipe", "dp", "expert"),
        P("pipe", "dp", "expert"),
    )
    return jax.shard_map(body, mesh=mesh, in_specs=in_specs, out_specs=out_specs, check_vma=False)
```

profile of v0, /device:TPU:1, one launch (start us, length us, event | category | flops | bytes accessed | tf_op | source)
XLA Modules:
  0.0 624.1 jit_solution(5665238719745592529)
XLA Ops:
  10.5 19.3 %all-to-all-start = ((bf16[64,1,6]{2,1,0:T(2,128)(2,1)}), bf16[64,1,6]{2,1,0:T(2,128)(2,1)S(1)}, u32[]{:S(2)}, u32[]{:S(2)}) async-start(bf16[64,1,6]{2,1,0:T(2,128)(2,1)} %copy.49), calls=%async_computation | async-start | bytes 65536 | tf_op jit(solution)/shard_map/all_to_all | solution.py:75
  31.1 11.9 %all-to-all-done = bf16[64,1,6]{2,1,0:T(2,128)(2,1)S(1)} async-done(((bf16[64,1,6]{2,1,0:T(2,128)(2,1)}), bf16[64,1,6]{2,1,0:T(2,128)(2,1)S(1)}, u32[]{:S(2)}, u32[]{:S(2)}) %all-to-all-start) | async-done | bytes 800 | tf_op jit(solution)/shard_map/all_to_all | solution.py:75
  45.0 5.8 all-to-all-start.1
  51.2 158.9 %all-to-all-done.1 = bf16[64,6,3584]{2,1,0:T(8,128)(2,1)} async-done(((bf16[64,6,3584]{2,1,0:T(8,128)(2,1)}), bf16[64,6,3584]{2,1,0:T(8,128)(2,1)}, u32[]{:S(2)}, u32[]{:S(2)}) %all-to-all-start.1) | async-done | bytes 2752544 | tf_op jit(solution)/shard_map/all_to_all | solution.py:72
  212.2 13.8 %all-to-all-start.2 = ((bf16[64,6,3584]{2,1,0:T(8,128)(2,1)}), bf16[64,6,3584]{2,1,0:T(8,128)(2,1)}, u32[]{:S(2)}, u32[]{:S(2)}) async-start(bf16[64,6,3584]{2,1,0:T(8,128)(2,1)} %bitcast.71), calls=%async_computation.2 | async-start | bytes 7340032 | tf_op jit(solution)/shard_map/all_to_all | solution.py:69
  226.0 13.6 %all_gather.11 = bf16[1,3584,128]{2,1,0:T(8,128)(2,1)} all-gather(bf16[1,896,128]{2,1,0:T(8,128)(2,1)S(1)} %copy-done.5), channel_id=1, replica_groups=mesh['pipe'=2,'expert'=64,'dp'=4] {'dp'}, dimensions={1}, use_global_device_ids=true | all-gather | bytes 1146880 | tf_op jit(solution)/shard_map/all_gather | solution.py:85
  239.6 12.5 %all_gather.10 = bf16[1,3584,128]{2,1,0:T(8,128)(2,1)} all-gather(bf16[1,896,128]{2,1,0:T(8,128)(2,1)S(1)} %copy-done.6), channel_id=1, replica_groups=mesh['pipe'=2,'expert'=64,'dp'=4] {'dp'}, dimensions={1}, use_global_device_ids=true | all-gather | bytes 1146880 | tf_op jit(solution)/shard_map/all_gather | solution.py:86
  252.1 12.8 %all_gather.9 = bf16[1,3584,128]{2,1,0:T(8,128)(2,1)} all-gather(bf16[1,896,128]{2,1,0:T(8,128)(2,1)S(1)} %copy-done.7), channel_id=1, replica_groups=mesh['pipe'=2,'expert'=64,'dp'=4] {'dp'}, dimensions={1}, use_global_device_ids=true | all-gather | bytes 1146880 | tf_op jit(solution)/shard_map/all_gather | solution.py:87
  264.9 4.7 multiply_convert_fusion
  269.7 5.5 convert_element_type.104
  275.1 109.9 %all-to-all-done.2 = bf16[64,6,3584]{2,1,0:T(8,128)(2,1)} async-done(((bf16[64,6,3584]{2,1,0:T(8,128)(2,1)}), bf16[64,6,3584]{2,1,0:T(8,128)(2,1)}, u32[]{:S(2)}, u32[]{:S(2)}) %all-to-all-start.2) | async-done | bytes 2752544 | tf_op jit(solution)/shard_map/all_to_all | solution.py:69
  385.0 4.0 reshape.129
  393.0 6.0 reshape.137
  399.0 3.8 fusion.3
  403.6 13.7 %all-to-all-start.4 = ((bf16[64,1,6]{2,1,0:T(2,128)(2,1)}), bf16[64,1,6]{2,1,0:T(2,128)(2,1)S(1)}, u32[]{:S(2)}, u32[]{:S(2)}) async-start(bf16[64,1,6]{2,1,0:T(2,128)(2,1)} %convert_element_type.126), calls=%async_computation.4 | async-start | bytes 65536 | tf_op jit(solution)/shard_map/all_to_all | solution.py:115
  421.9 5.4 convert_element_type.109
  427.3 3.0 all-to-all-done.4
  430.4 11.6 %all-to-all-start.3 = ((bf16[64,6,3584]{2,1,0:T(8,128)(2,1)}), bf16[64,6,3584]{2,1,0:T(8,128)(2,1)}, u32[]{:S(2)}, u32[]{:S(2)}) async-start(bf16[64,6,3584]{2,1,0:T(8,128)(2,1)} %convert_element_type.109), calls=%async_computation.3 | async-start | bytes 7340032 | tf_op jit(solution)/shard_map/all_to_all | solution.py:108
  443.6 3.3 convolution_convert_fusion
  447.2 2.7 copy.55
  450.9 43.9 %reduce-scatter.4.cloned.1.call-done = bf16[896,384]{1,0:T(8,128)(2,1)} async-done(((bf16[3584,384]{1,0:T(8,128)(2,1)}), bf16[896,384]{1,0:T(8,128)(2,1)}) %reduce-scatter.4.cloned.1.call-update) | async-done | bytes 688144
  496.3 105.0 %all-to-all-done.3 = bf16[64,6,3584]{2,1,0:T(8,128)(2,1)} async-done(((bf16[64,6,3584]{2,1,0:T(8,128)(2,1)}), bf16[64,6,3584]{2,1,0:T(8,128)(2,1)}, u32[]{:S(2)}, u32[]{:S(2)}) %all-to-all-start.3) | async-done | bytes 2752544 | tf_op jit(solution)/shard_map/all_to_all | solution.py:108
  601.3 2.9 convert_reduce_fusion
  604.6 9.0 %collective-permute-start = (bf16[1,8,3584]{2,1,0:T(8,128)(2,1)S(1)}, bf16[1,8,3584]{2,1,0:T(8,128)(2,1)S(1)}, u32[]{:S(2)}, u32[]{:S(2)}) collective-permute-start(bf16[1,8,3584]{2,1,0:T(8,128)(2,1)S(1)} %fusion.1), channel_id=1, source_target_pairs={{256,0},{0,256},{257,1},{1,257},{258,2},{2,258},{259,3},{3,259},{2... | collective-permute-start | bytes 172040 | tf_op jit(solution)/shard_map/ppermute | solution.py:13
  (70 shorter events, 27.0 us)
Async XLA Ops:
  7.2 23.5 %copy-start = (bf16[1,8,3584]{2,1,0:T(8,128)(2,1)S(1)}, bf16[1,8,3584]{2,1,0:T(8,128)(2,1)}, u32[]{:S(2)}) copy-start(bf16[1,8,3584]{2,1,0:T(8,128)(2,1)} %param.8) | copy-start | bytes 172036
  10.5 32.5 %all-to-all-start = ((bf16[64,1,6]{2,1,0:T(2,128)(2,1)}), bf16[64,1,6]{2,1,0:T(2,128)(2,1)S(1)}, u32[]{:S(2)}, u32[]{:S(2)}) async-start(bf16[64,1,6]{2,1,0:T(2,128)(2,1)} %copy.49), calls=%async_computation | async-start | bytes 65536 | tf_op jit(solution)/shard_map/all_to_all | solution.py:75
  45.0 5.8 copy-start.8
  45.0 165.1 %all-to-all-start.1 = ((bf16[64,6,3584]{2,1,0:T(8,128)(2,1)}), bf16[64,6,3584]{2,1,0:T(8,128)(2,1)}, u32[]{:S(2)}, u32[]{:S(2)}) async-start(bf16[64,6,3584]{2,1,0:T(8,128)(2,1)} %bitcast.72), calls=%async_computation.1 | async-start | bytes 7340032 | tf_op jit(solution)/shard_map/all_to_all | solution.py:72
  212.2 13.8 %copy-start.5 = (bf16[1,896,128]{2,1,0:T(8,128)(2,1)S(1)}, bf16[1,896,128]{2,1,0:T(8,128)(2,1)}, u32[]{:S(2)}) copy-start(bf16[1,896,128]{2,1,0:T(8,128)(2,1)} %param.11) | copy-start | bytes 688132
  212.2 27.4 %copy-start.6 = (bf16[1,896,128]{2,1,0:T(8,128)(2,1)S(1)}, bf16[1,896,128]{2,1,0:T(8,128)(2,1)}, u32[]{:S(2)}) copy-start(bf16[1,896,128]{2,1,0:T(8,128)(2,1)} %param.12) | copy-start | bytes 688132
  212.2 39.9 %copy-start.7 = (bf16[1,896,128]{2,1,0:T(8,128)(2,1)S(1)}, bf16[1,896,128]{2,1,0:T(8,128)(2,1)}, u32[]{:S(2)}) copy-start(bf16[1,896,128]{2,1,0:T(8,128)(2,1)} %param.13) | copy-start | bytes 688132
  212.2 172.8 %all-to-all-start.2 = ((bf16[64,6,3584]{2,1,0:T(8,128)(2,1)}), bf16[64,6,3584]{2,1,0:T(8,128)(2,1)}, u32[]{:S(2)}, u32[]{:S(2)}) async-start(bf16[64,6,3584]{2,1,0:T(8,128)(2,1)} %bitcast.71), calls=%async_computation.2 | async-start | bytes 7340032 | tf_op jit(solution)/shard_map/all_to_all | solution.py:69
  389.0 2.2 copy-start.1
  389.0 2.3 copy-start.2
  389.0 3.1 copy-start.3
  403.6 26.7 %all-to-all-start.4 = ((bf16[64,1,6]{2,1,0:T(2,128)(2,1)}), bf16[64,1,6]{2,1,0:T(2,128)(2,1)S(1)}, u32[]{:S(2)}, u32[]{:S(2)}) async-start(bf16[64,1,6]{2,1,0:T(2,128)(2,1)} %convert_element_type.126), calls=%async_computation.4 | async-start | bytes 65536 | tf_op jit(solution)/shard_map/all_to_all | solution.py:115
  417.3 2.2 copy-start.4
  430.4 170.9 %all-to-all-start.3 = ((bf16[64,6,3584]{2,1,0:T(8,128)(2,1)}), bf16[64,6,3584]{2,1,0:T(8,128)(2,1)}, u32[]{:S(2)}, u32[]{:S(2)}) async-start(bf16[64,6,3584]{2,1,0:T(8,128)(2,1)} %convert_element_type.109), calls=%async_computation.3 | async-start | bytes 7340032 | tf_op jit(solution)/shard_map/all_to_all | solution.py:108
  442.0 52.8 %reduce-scatter.4.cloned.1.call-start = ((), (), s32[]{:S(2)}) async-start(), calls=%async_computation.6 | async-start | bytes 3440640
  604.6 12.0 %collective-permute-start = (bf16[1,8,3584]{2,1,0:T(8,128)(2,1)S(1)}, bf16[1,8,3584]{2,1,0:T(8,128)(2,1)S(1)}, u32[]{:S(2)}, u32[]{:S(2)}) collective-permute-start(bf16[1,8,3584]{2,1,0:T(8,128)(2,1)S(1)} %fusion.1), channel_id=1, source_target_pairs={{256,0},{0,256},{257,1},{1,257},{258,2},{2,258},{259,3},{3,259},{2... | collective-permute-start | bytes 172040 | tf_op jit(solution)/shard_map/ppermute | solution.py:13
Sparse Core Ops, SparseCore 0:
  450.0 44.7 reduce-scatter.3
where the time goes:
time: 625 us; the launch traced here: 624 us
  waiting for transfers between devices  433 us (69%)
  starting transfers between devices  73.1 us (12%)
  blocking collectives  38.9 us (6%)
  local copies, waits for them, and re-layouts  37.1 us (6%)
  matrix products  19 us (3%)
  between operations  14.3 us (2%)
  other arithmetic  9.14 us (1%)
    all_to_all x1, waiting for transfers between devices, body(): lax.all_to_all(replicate_slots(slot_cotangent), 'expert', split_axis=0, c...  159 us
    all_to_all x1, waiting for transfers between devices, body(): lax.all_to_all(replicate_slots(slot_inputs), 'expert', split_axis=0, conc...  110 us
    all_to_all x1, waiting for transfers between devices, body(): lax.all_to_all(input_rows.reshape(devices, capacity, model_width).astype(...  105 us
    unnamed x2, waiting for transfers between devices  43.9 us
    all_to_all x1, starting transfers between devices, body(): lax.all_to_all(replicate_slots(slot_weight), 'expert', split_axis=0, conc...  19.3 us
    all_to_all x1, starting transfers between devices, body(): lax.all_to_all(replicate_slots(slot_inputs), 'expert', split_axis=0, conc...  13.8 us
    all_to_all x1, starting transfers between devices, body(): lax.all_to_all(route_score.reshape(devices, capacity).astype(jnp.bfloat16...  13.7 us
    all_gather x1, blocking collectives, body(): lax.all_gather(w_gate, 'dp', axis=1, tiled=True)  13.6 us
  transfers between devices with their start and end apart: 7, of which 6 were waited for; matrix products, arithmetic and copies ran while one was open for 6% of the time, Pallas kernels for 0%

commit v1 on v0

v1 whole, which is shorter than its diff:
```python
import jax
import jax.numpy as jnp
from jax import lax
from jax.sharding import PartitionSpec as P

BF16 = jnp.bfloat16
F32 = jnp.float32
contract_first = (((0,), (0,)), ((), ()))
contract_last = (((1,), (1,)), ((), ()))


def exchange(blocks, axis, groups=None):
    return lax.all_to_all(blocks, axis, 0, 0, axis_index_groups=groups, tiled=True)


def body(tokens, grad_out, routes, combine, w_gate, w_up, w_down):
    tok, width = tokens.shape[1:]
    experts = 8
    n_x = lax.axis_size("dp")
    n_e = lax.axis_size("expert")
    n_z = 2 * (n_e // experts)
    n_y = n_e // n_z
    q = 4
    r = n_z // q
    cols = width // n_x
    ff = w_gate.shape[2]
    rows = n_z * n_x * tok
    along_y = [[y * n_z + z for y in range(n_y)] for z in range(n_z)]
    along_z = [[y * n_z + z for z in range(n_z)] for y in range(n_y)]
    near_z = [[y * n_z + a * r + b for b in range(r)] for y in range(n_y) for a in range(q)]
    far_z = [[y * n_z + a * r + b for a in range(q)] for y in range(n_y) for b in range(r)]
    upper_half = lax.axis_index("expert") % n_z >= n_z // 2

    own_weights = jnp.concatenate([w_gate[0], w_up[0], w_down[0]], axis=1)
    weights = lax.all_gather(own_weights, "expert", axis_index_groups=along_y)

    both = jnp.concatenate([tokens[0], grad_out[0]], axis=0).reshape(2 * tok, n_x, cols)
    both = exchange(both.transpose(1, 0, 2), "dp")
    x_rows = both[:, :tok].reshape(n_x * tok, cols)
    g_rows = both[:, tok:].reshape(n_x * tok, cols)
    chosen = routes[0][:, :, None] == jnp.arange(experts, dtype=jnp.int32)
    dense = jnp.sum(jnp.where(chosen, combine[0].astype(F32)[:, :, None], 0.0), axis=1)
    dense = jnp.pad(dense.astype(BF16), ((0, (n_x - 1) * tok), (0, 0)))
    g_rows = jnp.concatenate([g_rows, dense], axis=1)
    x_all = lax.all_gather(x_rows, "expert", axis_index_groups=along_z, tiled=True)
    g_all = lax.all_gather(g_rows, "expert", axis_index_groups=along_z, tiled=True)
    route_weight = g_all.reshape(n_z, n_x * tok, -1)[:, :tok, cols:].astype(F32)
    route_weight = route_weight.reshape(n_z * tok, n_y, 2)
    route_weight = jnp.where(upper_half, route_weight[:, :, 1], route_weight[:, :, 0])
    route_weight = route_weight.T[:, :, None]
    g_all = g_all[:, :cols]

    partial = []
    for y in range(n_y):
        first = jnp.dot(x_all, weights[y, :, : 2 * ff], preferred_element_type=F32)
        second = jnp.dot(g_all, weights[y, :, 2 * ff :], preferred_element_type=F32)
        partial.append(jnp.concatenate([first.astype(BF16), second.astype(BF16)], axis=1))
    partial = jnp.stack(partial).reshape(n_y, n_z, n_x, tok, 3 * ff).transpose(2, 0, 1, 3, 4)
    partial = exchange(partial, "dp")
    full = jnp.sum(partial.astype(F32), axis=0).reshape(n_y, n_z * tok, 3 * ff)
    gate = full[:, :, :ff]
    up = full[:, :, ff : 2 * ff]
    down_grad = full[:, :, 2 * ff :]
    sig = jax.nn.sigmoid(gate)
    act = gate * sig
    hidden = act * up
    score = jnp.sum(hidden * down_grad, axis=2)
    hidden_grad = down_grad * route_weight
    gate_grad = hidden_grad * up * sig * (1.0 + gate * (1.0 - sig))
    up_grad = hidden_grad * act
    grads = jnp.concatenate(
        [gate_grad.astype(BF16), up_grad.astype(BF16), (hidden * route_weight).astype(BF16)], axis=2
    )
    grads = exchange(jnp.broadcast_to(grads[None], (n_x,) + grads.shape), "dp")
    grads = grads.reshape(n_x, n_y, n_z, tok, 3 * ff).transpose(1, 2, 0, 3, 4)
    grads = grads.reshape(n_y, rows, 3 * ff)

    weight_grads = []
    for y in range(n_y):
        first = lax.dot_general(
            x_all, grads[y, :, : 2 * ff], contract_first, preferred_element_type=F32
        )
        second = lax.dot_general(
            g_all, grads[y, :, 2 * ff :], contract_first, preferred_element_type=F32
        )
        weight_grads.append(jnp.concatenate([first.astype(BF16), second.astype(BF16)], axis=1))
    weight_grads = lax.psum_scatter(
        jnp.stack(weight_grads), "expert", scatter_dimension=0, axis_index_groups=along_y
    ).astype(F32)

    input_grad = jnp.zeros((rows, cols), F32)
    for y in range(n_y):
        input_grad = input_grad + lax.dot_general(
            grads[y, :, : 2 * ff],
            weights[y, :, : 2 * ff],
            contract_last,
            preferred_element_type=F32,
        )
    score = score.reshape(n_y, n_z, tok).transpose(1, 2, 0)
    score = jnp.stack(
        [jnp.where(upper_half, 0.0, score), jnp.where(upper_half, score, 0.0)], axis=3
    )
    score = score.reshape(n_z, tok, experts).astype(BF16)
    score = jnp.pad(score, ((0, 0), (0, (n_x - 1) * tok), (0, 128 - experts)))
    back = jnp.concatenate(
        [input_grad.astype(BF16).reshape(n_z, n_x * tok, cols), score], axis=2
    )
    back = back.reshape((q, r) + back.shape[1:]).transpose(1, 0, 2, 3)
    back = jnp.sum(exchange(back, "expert", near_z).astype(F32), axis=0).astype(BF16)
    back = jnp.sum(exchange(back, "expert", far_z).astype(F32), axis=0)
    score = back[:tok, cols : cols + experts]
    grad_combine = jnp.sum(jnp.where(chosen, score[:, None, :], 0.0), axis=2)[None]
    passed = exchange(back[:, :cols].astype(BF16).reshape(n_x, tok, cols), "dp")
    passed = passed.transpose(1, 0, 2).reshape(1, tok, width)
    sections = lax.axis_size("pipe")
    passed = lax.ppermute(passed, "pipe", [(s, (s - 1) % sections) for s in range(sections)])
    return (
        passed,
        grad_combine,
        weight_grads[None, :, :ff],
        weight_grads[None, :, ff : 2 * ff],
        weight_grads[None, :, 2 * ff :],
    )


def solution(mesh):
    row_spec = P("pipe", ("expert", "dp"), None)
    weight_spec = P("pipe", "dp", "expert")
    in_specs = (row_spec,) * 4 + (weight_spec,) * 3
    out_specs = (row_spec,) * 2 + (weight_spec,) * 3
    return jax.shard_map(body, mesh=mesh, in_specs=in_specs, out_specs=out_specs, check_vma=False)
```

time: 625 us -> 232 us (0.37)
  waiting for transfers between devices: 433 us -> 37.3 us
  blocking collectives: 38.9 us -> 101 us
  starting transfers between devices: 73.1 us -> 43.4 us
  local copies, waits for them, and re-layouts: 37.1 us -> 10.1 us
    all_to_all x5 -> x4, waiting for transfers between devices: 389 us -> 37.1 us  [exchange(): lax.all_to_all(blocks, axis, 0, 0, axis_index_groups=groups, tiled=True)]
    all_to_all x5 -> x4, starting transfers between devices: 64.1 us -> 15.2 us  [exchange(): lax.all_to_all(blocks, axis, 0, 0, axis_index_groups=groups, tiled=True)]
    unnamed x2, waiting for transfers between devices: 43.9 us -> 0.03 us
    all_to_all x0 -> x2, blocking collectives: none -> 38.5 us  [exchange(): lax.all_to_all(blocks, axis, 0, 0, axis_index_groups=groups, tiled=True)]
    all_gather x3 -> x2, blocking collectives: 38.9 us -> 62.1 us  [the longest x1 35.9 us: body(): lax.all_gather(x_rows, 'expert', axis_index_groups=along_z, tiled=True)]
    ppermute x1, starting transfers between devices: 9 us -> 28.1 us  [body(): lax.ppermute(passed, 'pipe', [(s, (s - 1) % sections) for s in range(sect...]
    convert_element_type x5 -> x0, local copies, waits for them, and re-layouts: 17.8 us -> none  [the longest x1 5.96 us: body(): row_cotangent.astype(jnp.float32)]
    dot_general x14 -> x20, matrix products: 19 us -> 15.5 us  [the longest x4 6.05 us: body(): lax.dot_general(grads[y, :, :2 * ff], weights[y, :, :2 * ff], contract_la...]
  transfers between devices with their start and end apart: 7 -> 7, of which waited for: 6 -> 5; matrix products, arithmetic and copies ran while one was open for 6% -> 3% of each run, Pallas kernels for 0% -> 0%
where the time goes in v1:
time: 232 us; the launch traced here: 229 us
  blocking collectives  101 us (44%)
  starting transfers between devices  43.4 us (19%)
  waiting for transfers between devices  37.3 us (16%)
  matrix products  15.5 us (7%)
  between operations  14.5 us (6%)
  local copies, waits for them, and re-layouts  10.1 us (4%)
  other arithmetic  8.15 us (4%)
    all_to_all x2, blocking collectives, exchange(): lax.all_to_all(blocks, axis, 0, 0, axis_index_groups=groups, tiled=True)  38.5 us
    all_to_all x4, waiting for transfers between devices, exchange(): lax.all_to_all(blocks, axis, 0, 0, axis_index_groups=groups, tiled=True)  37.1 us
    all_gather x1, blocking collectives, body(): lax.all_gather(x_rows, 'expert', axis_index_groups=along_z, tiled=True)  35.9 us
    ppermute x1, starting transfers between devices, body(): lax.ppermute(passed, 'pipe', [(s, (s - 1) % sections) for s in range(sect...  28.1 us
    all_gather x1, blocking collectives, body(): lax.all_gather(g_rows, 'expert', axis_index_groups=along_z, tiled=True)  26.2 us
    all_to_all x4, starting transfers between devices, exchange(): lax.all_to_all(blocks, axis, 0, 0, axis_index_groups=groups, tiled=True)  15.2 us
    dot_general x4, matrix products, body(): lax.dot_general(grads[y, :, :2 * ff], weights[y, :, :2 * ff], contract_la...  6.05 us
    unnamed x24, local copies, waits for them, and re-layouts  4.97 us
  transfers between devices with their start and end apart: 7, of which 5 were waited for; matrix products, arithmetic and copies ran while one was open for 3% of the time, Pallas kernels for 0%

profile of v1, /device:TPU:1, one launch (start us, length us, event | category | flops | bytes accessed | tf_op | source)
XLA Modules:
  0.0 229.5 jit_solution(15771802105247980246)
XLA Ops:
  7.3 2.1 pad_maximum_fusion.2
  10.1 4.8 %all-to-all-start = ((bf16[4,16,896]{2,1,0:T(8,128)(2,1)}), bf16[4,16,896]{2,1,0:T(8,128)(2,1)S(1)}, u32[]{:S(2)}, u32[]{:S(2)}) async-start(bf16[4,16,896]{2,1,0:T(8,128)(2,1)} %maximum_bitcast_fusion.5), calls=%async_computation | async-start | bytes 229376 | tf_op jit(solution)/shard_map/all_to_all | solution.py:13
  15.0 4.6 %all-to-all-done = bf16[4,16,896]{2,1,0:T(8,128)(2,1)S(1)} async-done(((bf16[4,16,896]{2,1,0:T(8,128)(2,1)}), bf16[4,16,896]{2,1,0:T(8,128)(2,1)S(1)}, u32[]{:S(2)}, u32[]{:S(2)}) %all-to-all-start) | async-done | bytes 114720 | tf_op jit(solution)/shard_map/all_to_all | solution.py:13
  19.7 35.9 %all_gather.12 = bf16[512,896]{1,0:T(8,128)(2,1)S(1)} all-gather(bf16[32,896]{1,0:T(8,128)(2,1)S(1)} %get-tuple-element.42), channel_id=1, replica_groups={{0,4,8,12,16,20,24,28,32,36,40,44,48,52,56,60},{64,68,72,76,80,84,88,92..., dimensions={0}, use_global_device_ids=true | all-gather | bytes 974848 | tf_op jit(solution)/shard_map/all_gather | solution.py:45
  55.6 26.2 %all_gather.15 = bf16[512,904]{1,0:T(8,128)(2,1)S(1)} all-gather(bf16[32,904]{1,0:T(8,128)(2,1)S(1)} %fusion.13), channel_id=1, replica_groups={{0,4,8,12,16,20,24,28,32,36,40,44,48,52,56,60},{64,68,72,76,80,84,88,92..., dimensions={0}, use_global_device_ids=true | all-gather | bytes 983552 | tf_op jit(solution)/shard_map/all_gather | solution.py:46
  81.8 1.8 convolution_convert_fusion.15
  83.6 1.4 convolution_convert_fusion.14
  89.1 1.4 copy.79
  90.5 3.6 %all-to-all-start.1 = ((bf16[4,4,16,8,384]{4,3,2,1,0:T(8,128)(2,1)}), bf16[4,4,16,8,384]{4,3,2,1,0:T(8,128)(2,1)S(1)}, u32[]{:S(2)}, u32[]{:S(2)}) async-start(bf16[4,4,16,8,384]{4,3,2,1,0:T(8,128)(2,1)} %copy.79), calls=%async_computation.1 | async-start | bytes 3145728 | tf_op jit(solution)/shard_map/all_to_all | solution.py:13
  94.5 12.2 %all-to-all-done.1 = bf16[4,4,16,8,384]{4,3,2,1,0:T(8,128)(2,1)S(1)} async-done(((bf16[4,4,16,8,384]{4,3,2,1,0:T(8,128)(2,1)}), bf16[4,4,16,8,384]{4,3,2,1,0:T(8,128)(2,1)S(1)}, u32[]{:S(2)}, u32[]{:S(2)}) %all-to-all-start.1) | async-done | bytes 1572896 | tf_op jit(solution)/shard_map/all_to_all | solution.py:13
  107.2 1.4 broadcast_in_dim.52
  108.6 3.6 %all-to-all-start.2 = ((bf16[4,4,128,384]{3,2,1,0:T(8,128)(2,1)}), bf16[4,4,128,384]{3,2,1,0:T(8,128)(2,1)S(1)}, u32[]{:S(2)}, u32[]{:S(2)}) async-start(bf16[4,4,128,384]{3,2,1,0:T(8,128)(2,1)} %broadcast_in_dim.52), calls=%async_computation.2 | async-start | bytes 3145728 | tf_op jit(solution)/shard_map/all_to_all | solution.py:13
  112.8 15.9 %all-to-all-done.2 = bf16[4,4,128,384]{3,2,1,0:T(8,128)(2,1)S(1)} async-done(((bf16[4,4,128,384]{3,2,1,0:T(8,128)(2,1)}), bf16[4,4,128,384]{3,2,1,0:T(8,128)(2,1)S(1)}, u32[]{:S(2)}, u32[]{:S(2)}) %all-to-all-start.2) | async-done | bytes 1572896 | tf_op jit(solution)/shard_map/all_to_all | solution.py:13
  133.5 1.5 fusion
  135.3 1.8 pad_maximum_fusion
  137.1 1.5 fusion.1
  138.6 1.5 fusion.2
  140.1 1.6 add_convert_fusion
  141.8 17.2 %all_to_all.30 = bf16[4,4,32,1024]{3,2,1,0:T(8,128)(2,1)S(1)} all-to-all(bf16[4,4,32,1024]{3,2,1,0:T(8,128)(2,1)S(1)} %copy_bitcast_fusion), channel_id=1, replica_groups={{0,4,8,12},{16,20,24,28},{32,36,40,44},{48,52,56,60},{64,68,72,76},{80,..., dimensions={0} | all-to-all | bytes 2097152 | tf_op jit(solution)/shard_map/all_to_all | solution.py:13
  159.2 21.3 %all_to_all.31 = bf16[4,32,1024]{2,1,0:T(8,128)(2,1)S(1)} all-to-all(bf16[4,32,1024]{2,1,0:T(8,128)(2,1)S(1)} %reduce_sum.60), channel_id=1, replica_groups={{0,16,32,48},{4,20,36,52},{8,24,40,56},{12,28,44,60},{64,80,96,112},{68..., dimensions={0} | all-to-all | bytes 524288 | tf_op jit(solution)/shard_map/all_to_all | solution.py:13
  181.2 3.3 %all-to-all-start.5 = ((bf16[4,8,896]{2,1,0:T(8,128)(2,1)}), bf16[4,8,896]{2,1,0:T(8,128)(2,1)S(1)}, u32[]{:S(2)}, u32[]{:S(2)}) async-start(bf16[4,8,896]{2,1,0:T(8,128)(2,1)} %fusion.14), calls=%async_computation.5 | async-start | bytes 114688 | tf_op jit(solution)/shard_map/all_to_all | solution.py:13
  184.5 4.4 %all-to-all-done.5 = bf16[4,8,896]{2,1,0:T(8,128)(2,1)S(1)} async-done(((bf16[4,8,896]{2,1,0:T(8,128)(2,1)}), bf16[4,8,896]{2,1,0:T(8,128)(2,1)S(1)}, u32[]{:S(2)}, u32[]{:S(2)}) %all-to-all-start.5) | async-done | bytes 57376 | tf_op jit(solution)/shard_map/all_to_all | solution.py:13
  188.9 28.1 %collective-permute-start = (bf16[1,8,3584]{2,1,0:T(8,128)(2,1)S(1)}, bf16[1,8,3584]{2,1,0:T(8,128)(2,1)S(1)}, u32[]{:S(2)}, u32[]{:S(2)}) collective-permute-start(bf16[1,8,3584]{2,1,0:T(8,128)(2,1)S(1)} %bitcast.170), channel_id=1, source_target_pairs={{0,256},{256,0},{1,257},{257,1},{2,258},{258,2},{3,259},{259,3},{4... | collective-permute-start | bytes 172040 | tf_op jit(solution)/shard_map/ppermute | solution.py:116
  217.8 1.2 bitcast_convert_fusion
  (83 shorter events, 16.8 us)
Async XLA Ops:
  7.2 2.2 copy-start.6
  7.2 2.2 copy-start.5
  7.2 7.7 %copy-start.8 = (bf16[1,8,4]{1,2,0:T(4,128)(2,1)S(1)}, bf16[1,8,4]{1,2,0:T(4,128)(2,1)}, u32[]{:S(2)}) copy-start(bf16[1,8,4]{1,2,0:T(4,128)(2,1)} %param.10) | copy-start | bytes 196
  7.2 7.7 %copy-start.7 = (s32[1,8,4]{1,2,0:T(4,128)S(1)}, s32[1,8,4]{1,2,0:T(4,128)}, u32[]{:S(2)}) copy-start(s32[1,8,4]{1,2,0:T(4,128)} %param.9) | copy-start | bytes 388
  7.2 74.6 %all-gather.3.cloned.1.call-start = ((), (), s32[]{:S(2)}) async-start(), calls=%async_computation.8 | async-start | bytes 3440640 | tf_op jit(solution)/shard_map/all_gather | solution.py:35
  10.1 9.6 %all-to-all-start = ((bf16[4,16,896]{2,1,0:T(8,128)(2,1)}), bf16[4,16,896]{2,1,0:T(8,128)(2,1)S(1)}, u32[]{:S(2)}, u32[]{:S(2)}) async-start(bf16[4,16,896]{2,1,0:T(8,128)(2,1)} %maximum_bitcast_fusion.5), calls=%async_computation | async-start | bytes 229376 | tf_op jit(solution)/shard_map/all_to_all | solution.py:13
  55.6 31.8 %copy-start.3 = (bf16[512,896]{1,0:T(8,128)(2,1)}, bf16[512,896]{1,0:T(8,128)(2,1)S(1)}, u32[]{:S(2)}) copy-start(bf16[512,896]{1,0:T(8,128)(2,1)S(1)} %all_gather.12) | copy-start | bytes 2752516
  81.8 12.3 %copy-start.1 = (bf16[512,904]{1,0:T(8,128)(2,1)}, bf16[512,904]{1,0:T(8,128)(2,1)S(1)}, u32[]{:S(2)}) copy-start(bf16[512,904]{1,0:T(8,128)(2,1)S(1)} %all_gather.15) | copy-start | bytes 2777092
  81.8 3.2 %copy-start = (bf16[3584,384]{1,0:T(8,128)(2,1)S(1)}, bf16[3584,384]{1,0:T(8,128)(2,1)}, u32[]{:S(2)}) copy-start(bf16[3584,384]{1,0:T(8,128)(2,1)} %all-gather.3.cloned.1.call-done) | copy-start | bytes 8257540
  90.5 16.1 %all-to-all-start.1 = ((bf16[4,4,16,8,384]{4,3,2,1,0:T(8,128)(2,1)}), bf16[4,4,16,8,384]{4,3,2,1,0:T(8,128)(2,1)S(1)}, u32[]{:S(2)}, u32[]{:S(2)}) async-start(bf16[4,4,16,8,384]{4,3,2,1,0:T(8,128)(2,1)} %copy.79), calls=%async_computation.1 | async-start | bytes 3145728 | tf_op jit(solution)/shard_map/all_to_all | solution.py:13
  108.6 20.1 %all-to-all-start.2 = ((bf16[4,4,128,384]{3,2,1,0:T(8,128)(2,1)}), bf16[4,4,128,384]{3,2,1,0:T(8,128)(2,1)S(1)}, u32[]{:S(2)}, u32[]{:S(2)}) async-start(bf16[4,4,128,384]{3,2,1,0:T(8,128)(2,1)} %broadcast_in_dim.52), calls=%async_computation.2 | async-start | bytes 3145728 | tf_op jit(solution)/shard_map/all_to_all | solution.py:13
  112.2 105.6 %reduce-scatter.2.cloned.1.call-start = ((), (), s32[]{:S(2)}) async-start(), calls=%async_computation.7 | async-start | bytes 3440640 | tf_op jit(solution)/shard_map/reduce_scatter | solution.py:87
  128.7 1.2 copy-start.4
  129.9 1.2 copy-start.2
  181.2 7.7 %all-to-all-start.5 = ((bf16[4,8,896]{2,1,0:T(8,128)(2,1)}), bf16[4,8,896]{2,1,0:T(8,128)(2,1)S(1)}, u32[]{:S(2)}, u32[]{:S(2)}) async-start(bf16[4,8,896]{2,1,0:T(8,128)(2,1)} %fusion.14), calls=%async_computation.5 | async-start | bytes 114688 | tf_op jit(solution)/shard_map/all_to_all | solution.py:13
  188.9 28.9 %collective-permute-start = (bf16[1,8,3584]{2,1,0:T(8,128)(2,1)S(1)}, bf16[1,8,3584]{2,1,0:T(8,128)(2,1)S(1)}, u32[]{:S(2)}, u32[]{:S(2)}) collective-permute-start(bf16[1,8,3584]{2,1,0:T(8,128)(2,1)S(1)} %bitcast.170), channel_id=1, source_target_pairs={{0,256},{256,0},{1,257},{257,1},{2,258},{258,2},{3,259},{259,3},{4... | collective-permute-start | bytes 172040 | tf_op jit(solution)/shard_map/ppermute | solution.py:116
Sparse Core Ops, SparseCore 0:
  10.1 49.2 all-gather.2
  137.2 55.5 reduce-scatter.1

commit v2 on v1

v2 whole, which is shorter than its diff:
```python
import jax
import jax.numpy as jnp
from jax import lax
from jax.sharding import PartitionSpec as P

BF16 = jnp.bfloat16
F32 = jnp.float32
contract_first = (((0,), (0,)), ((), ()))
contract_last = (((1,), (1,)), ((), ()))


def exchange(blocks, axis, groups=None):
    return lax.all_to_all(blocks, axis, 0, 0, axis_index_groups=groups, tiled=True)


def body(tokens, grad_out, routes, combine, w_gate, w_up, w_down):
    tok, width = tokens.shape[1:]
    experts = 8
    n_x = lax.axis_size("dp")
    n_e = lax.axis_size("expert")
    n_z = 2 * (n_e // experts)
    n_y = n_e // n_z
    half = n_z // 2
    quarter = half // 2
    cols = width // n_x
    ff = w_gate.shape[2]
    wide = n_y * ff
    along_y = [[y * n_z + z for y in range(n_y)] for z in range(n_z)]
    same_parity = [[y * n_z + 2 * i + p for i in range(half)] for y in range(n_y) for p in range(2)]
    up_z = [(y * n_z + z, y * n_z + (z + 1) % n_z) for y in range(n_y) for z in range(n_z)]
    down_z = [(b, a) for a, b in up_z]
    upper_half = lax.axis_index("expert") % n_z >= half

    def swap_parity(blocks):
        low = lax.ppermute(blocks[:quarter], "expert", up_z)
        high = lax.ppermute(blocks[quarter:], "expert", down_z)
        return low, high

    weights = jnp.stack([w_gate[0], w_up[0], w_down[0]])
    weights = lax.all_gather(weights, "expert", axis_index_groups=along_y)
    weights = weights.transpose(2, 1, 0, 3).reshape(cols, 3 * wide)

    both = jnp.concatenate([tokens[0], grad_out[0]], axis=0).reshape(2 * tok, n_x, cols)
    both = exchange(both.transpose(1, 0, 2), "dp")
    chosen = routes[0][:, :, None] == jnp.arange(experts, dtype=jnp.int32)
    dense = jnp.sum(jnp.where(chosen, combine[0].astype(F32)[:, :, None], 0.0), axis=1)
    dense = jnp.pad(dense.astype(BF16), ((0, (n_x - 1) * tok), (0, 0)))
    both = jnp.concatenate(
        [
            both[:, :tok].reshape(n_x * tok, cols),
            both[:, tok:].reshape(n_x * tok, cols),
            dense,
        ],
        axis=1,
    )
    own = lax.all_gather(both, "expert", axis_index_groups=same_parity)
    low, high = swap_parity(own)
    low, high, weights = lax.optimization_barrier((low, high, weights))
    rows = jnp.concatenate([own, low, high], axis=0).reshape(n_z, n_x, tok, -1)
    rows = rows.transpose(1, 0, 2, 3)
    route_weight = rows[0]
    rows = rows.reshape(n_x * n_z * tok, -1)
    x_rows = rows[:, :cols]
    g_rows = rows[:, cols : 2 * cols]

    first = jnp.dot(x_rows, weights[:, : 2 * wide], preferred_element_type=F32)
    second = jnp.dot(g_rows, weights[:, 2 * wide :], preferred_element_type=F32)
    partial = jnp.concatenate([first.astype(BF16), second.astype(BF16)], axis=1)
    partial = exchange(partial.reshape(n_x, n_z * tok, 3 * wide), "dp")
    full = jnp.sum(partial.astype(F32), axis=0)

    route_weight = route_weight.reshape(n_z * tok, -1)[:, 2 * cols : 2 * cols + experts]
    route_weight = route_weight.astype(F32).reshape(n_z * tok, n_y, 2)
    route_weight = jnp.where(upper_half, route_weight[:, :, 1], route_weight[:, :, 0])
    route_weight = jnp.broadcast_to(route_weight[:, :, None], (n_z * tok, n_y, ff))
    route_weight = route_weight.reshape(n_z * tok, wide)
    gate = full[:, :wide]
    up = full[:, wide : 2 * wide]
    down_grad = full[:, 2 * wide :]
    sig = jax.nn.sigmoid(gate)
    act = gate * sig
    hidden = act * up
    score = jnp.sum((hidden * down_grad).reshape(n_z, tok, n_y, ff), axis=3)
    score = jnp.stack(
        [jnp.where(upper_half, 0.0, score), jnp.where(upper_half, score, 0.0)], axis=3
    )
    score = score.reshape(n_z, tok, experts).astype(BF16)
    score = jnp.pad(score, ((0, 0), (0, (n_x - 1) * tok), (0, 128 - experts)))
    hidden_grad = down_grad * route_weight
    gate_grad = hidden_grad * up * sig * (1.0 + gate * (1.0 - sig))
    up_grad = hidden_grad * act
    grads = jnp.concatenate(
        [gate_grad.astype(BF16), up_grad.astype(BF16), (hidden * route_weight).astype(BF16)],
        axis=1,
    )
    grads = exchange(jnp.broadcast_to(grads[None], (n_x,) + grads.shape), "dp")
    grads = grads.reshape(n_x * n_z * tok, 3 * wide)

    back = lax.dot_general(
        grads[:, : 2 * wide], weights[:, : 2 * wide], contract_last, preferred_element_type=F32
    )
    back = back.astype(BF16).reshape(n_x, n_z, tok, cols).transpose(1, 0, 2, 3)
    back = jnp.concatenate([back.reshape(n_z, n_x * tok, cols), score], axis=2)
    low, high = swap_parity(back[half:])

    first = lax.dot_general(
        x_rows, grads[:, : 2 * wide], contract_first, preferred_element_type=F32
    )
    second = lax.dot_general(
        g_rows, grads[:, 2 * wide :], contract_first, preferred_element_type=F32
    )
    total = jnp.concatenate([first.astype(BF16), second.astype(BF16)], axis=1)
    total = total.reshape(cols, 3, n_y, ff).transpose(2, 1, 0, 3)
    low, high, total = lax.optimization_barrier((low, high, total))
    total = lax.psum_scatter(total, "expert", scatter_dimension=0, axis_index_groups=along_y)
    total = total.astype(F32)

    back = back[:half].astype(F32) + jnp.concatenate([low, high], axis=0).astype(F32)
    back = exchange(back.astype(BF16), "expert", same_parity)
    back = jnp.sum(back.astype(F32), axis=0)
    score = back[:tok, cols : cols + experts]
    grad_combine = jnp.sum(jnp.where(chosen, score[:, None, :], 0.0), axis=2)[None]
    passed = exchange(back[:, :cols].astype(BF16).reshape(n_x, tok, cols), "dp")
    passed = passed.transpose(1, 0, 2).reshape(1, tok, width)
    sections = lax.axis_size("pipe")
    passed = lax.ppermute(passed, "pipe", [(s, (s - 1) % sections) for s in range(sections)])
    return passed, grad_combine, total[0:1], total[1:2], total[2:3]


def solution(mesh):
    row_spec = P("pipe", ("expert", "dp"), None)
    weight_spec = P("pipe", "dp", "expert")
    in_specs = (row_spec,) * 4 + (weight_spec,) * 3
    out_specs = (row_spec,) * 2 + (weight_spec,) * 3
    return jax.shard_map(body, mesh=mesh, in_specs=in_specs, out_specs=out_specs, check_vma=False)
```

time: 232 us -> 200 us (0.86)
  blocking collectives: 101 us -> 65.9 us
  local copies, waits for them, and re-layouts: 10.1 us -> 20.3 us
  matrix products: 15.5 us -> 8.73 us
    all_gather x2 -> x1, blocking collectives: 62.1 us -> 36.9 us  [body(): own = lax.all_gather(both, 'expert', axis_index_groups=same_parity)]
    ppermute x0 -> x4, starting transfers between devices: none -> 14.3 us  [the longest x2 10.5 us: swap_parity(): high = lax.ppermute(blocks[quarter:], 'expert', down_z)]
    ppermute x1, starting transfers between devices: 28.1 us -> 14.6 us  [body(): lax.ppermute(passed, 'pipe', [(s, (s - 1) % sections) for s in range(sect...]
    all_to_all x2 -> x1, blocking collectives: 38.5 us -> 29 us  [exchange(): lax.all_to_all(blocks, axis, 0, 0, axis_index_groups=groups, tiled=True)]
    dot_general x20 -> x5, matrix products: 15.5 us -> 8.73 us  [the longest x1 2.61 us: body(): lax.dot_general(grads[:, :2 * wide], weights[:, :2 * wide], contract_last...]
    reshape x3 -> x4, local copies, waits for them, and re-layouts: 0.21 us -> 6.23 us  [the longest x2 6.14 us: body(): total = total.reshape(cols, 3, n_y, ff).transpose(2, 1, 0, 3)]
    all_to_all x4, waiting for transfers between devices: 37.1 us -> 33.8 us  [exchange(): lax.all_to_all(blocks, axis, 0, 0, axis_index_groups=groups, tiled=True)]
    transpose x2, local copies, waits for them, and re-layouts: 1.6 us -> 4.7 us  [the longest x1 4.55 us: body(): weights = weights.transpose(2, 1, 0, 3).reshape(cols, 3 * wide)]
  transfers between devices with their start and end apart: 7 -> 11, of which waited for: 5 -> 7; matrix products, arithmetic and copies ran while one was open for 3% -> 7% of each run, Pallas kernels for 0% -> 0%
where the time goes in v2:
time: 200 us; the launch traced here: 199 us
  blocking collectives  65.9 us (33%)
  starting transfers between devices  45.2 us (23%)
  waiting for transfers between devices  35.2 us (18%)
  local copies, waits for them, and re-layouts  20.3 us (10%)
  between operations  14.4 us (7%)
  matrix products  8.73 us (4%)
  other arithmetic  8.66 us (4%)
    all_gather x1, blocking collectives, body(): own = lax.all_gather(both, 'expert', axis_index_groups=same_parity)  36.9 us
    all_to_all x4, waiting for transfers between devices, exchange(): lax.all_to_all(blocks, axis, 0, 0, axis_index_groups=groups, tiled=True)  33.8 us
    all_to_all x1, blocking collectives, exchange(): lax.all_to_all(blocks, axis, 0, 0, axis_index_groups=groups, tiled=True)  29 us
    all_to_all x4, starting transfers between devices, exchange(): lax.all_to_all(blocks, axis, 0, 0, axis_index_groups=groups, tiled=True)  16.3 us
    ppermute x1, starting transfers between devices, body(): lax.ppermute(passed, 'pipe', [(s, (s - 1) % sections) for s in range(sect...  14.6 us
    ppermute x2, starting transfers between devices, swap_parity(): high = lax.ppermute(blocks[quarter:], 'expert', down_z)  10.5 us
    reshape x2, local copies, waits for them, and re-layouts, body(): total = total.reshape(cols, 3, n_y, ff).transpose(2, 1, 0, 3)  6.14 us
    unnamed x26, local copies, waits for them, and re-layouts  4.95 us
  transfers between devices with their start and end apart: 11, of which 7 were waited for; matrix products, arithmetic and copies ran while one was open for 7% of the time, Pallas kernels for 0%

profile of v2, /device:TPU:1, one launch (start us, length us, event | category | flops | bytes accessed | tf_op | source)
XLA Modules:
  0.0 198.5 jit_solution(6409615667528365360)
XLA Ops:
  7.3 2.1 %pad_maximum_fusion.2 = bf16[3,896,128]{2,1,0:T(8,128)(2,1)} fusion(bf16[1,896,128]{2,1,0:T(8,128)(2,1)} %param.13, bf16[1,896,128]{2,1,0:T(8,128)(2,1)} %param.12, bf16[1,896,128]{2,1,0:T(8,128)(2,1)} %param.11), kind=kLoop, calls=%fused_computation.27 | loop fusion | flops 688128 | bytes 1376256 | tf_op jit(solution)/shard_map/stack | solution.py:39
  10.1 4.8 %all-to-all-start = ((bf16[4,16,896]{2,1,0:T(8,128)(2,1)}), bf16[4,16,896]{2,1,0:T(8,128)(2,1)S(1)}, u32[]{:S(2)}, u32[]{:S(2)}) async-start(bf16[4,16,896]{2,1,0:T(8,128)(2,1)} %maximum_bitcast_fusion.1), calls=%async_computation | async-start | bytes 229376 | tf_op jit(solution)/shard_map/all_to_all | solution.py:13
  15.0 4.6 %all-to-all-done = bf16[4,16,896]{2,1,0:T(8,128)(2,1)S(1)} async-done(((bf16[4,16,896]{2,1,0:T(8,128)(2,1)}), bf16[4,16,896]{2,1,0:T(8,128)(2,1)S(1)}, u32[]{:S(2)}, u32[]{:S(2)}) %all-to-all-start) | async-done | bytes 114720 | tf_op jit(solution)/shard_map/all_to_all | solution.py:13
  19.7 36.9 %all-gather = bf16[256,1800]{1,0:T(8,128)(2,1)S(1)} all-gather(bf16[32,1800]{1,0:T(8,128)(2,1)S(1)} %fusion.23), channel_id=2, replica_groups={{0,8,16,24,32,40,48,56},{4,12,20,28,36,44,52,60},{64,72,80,88,96,104,11..., dimensions={0}, use_global_device_ids=true | all-gather | bytes 1036800 | tf_op jit(solution)/shard_map/all_gather | solution.py:56
  56.6 1.9 collective-permute-start
  58.6 4.6 %collective-permute-start.1 = (bf16[4,32,1800]{2,1,0:T(8,128)(2,1)S(1)}, bf16[4,32,1800]{2,1,0:T(8,128)(2,1)S(1)}, u32[]{:S(2)}, u32[]{:S(2)}) collective-permute-start(bf16[4,32,1800]{2,1,0:T(8,128)(2,1)S(1)} %bitcast.85), channel_id=1, source_target_pairs={{4,0},{8,4},{12,8},{16,12},{20,16},{24,20},{28,24},{32,28},{36,32}... | collective-permute-start | bytes 1382408 | tf_op jit(solution)/shard_map/ppermute | solution.py:36
  63.2 4.5 %copy.61 = bf16[896,3,4,128]{0,3,2,1:T(8,128)(2,1)} copy(bf16[896,3,4,128]{3,0,1,2:T(8,128)(2,1)} %bitcast.78) | data formatting | bytes 5505024 | tf_op jit(solution)/shard_map/transpose | solution.py:41
  71.2 2.3 %copy-done.2 = bf16[896,3,4,128]{0,3,2,1:T(8,128)(2,1)S(1)} copy-done((bf16[896,3,4,128]{0,3,2,1:T(8,128)(2,1)S(1)}, bf16[896,3,4,128]{0,3,2,1:T(8,128)(2,1)}, u32[]{:S(2)}) %copy-start.2) | copy-done | bytes 2752536
  75.5 1.3 pad_maximum_fusion.1
  76.8 3.6 %all-to-all-start.1 = ((bf16[4,128,1536]{2,1,0:T(8,128)(2,1)}), bf16[4,128,1536]{2,1,0:T(8,128)(2,1)S(1)}, u32[]{:S(2)}, u32[]{:S(2)}) async-start(bf16[4,128,1536]{2,1,0:T(8,128)(2,1)} %bitcast.73), calls=%async_computation.1 | async-start | bytes 3145728 | tf_op jit(solution)/shard_map/all_to_all | solution.py:13
  80.7 12.3 %all-to-all-done.1 = bf16[4,128,1536]{2,1,0:T(8,128)(2,1)S(1)} async-done(((bf16[4,128,1536]{2,1,0:T(8,128)(2,1)}), bf16[4,128,1536]{2,1,0:T(8,128)(2,1)S(1)}, u32[]{:S(2)}, u32[]{:S(2)}) %all-to-all-start.1) | async-done | bytes 1572896 | tf_op jit(solution)/shard_map/all_to_all | solution.py:13
  94.9 4.6 %all-to-all-start.2 = ((bf16[4,128,1536]{2,1,0:T(8,128)(2,1)}), bf16[4,128,1536]{2,1,0:T(8,128)(2,1)}, u32[]{:S(2)}, u32[]{:S(2)}) async-start(bf16[4,128,1536]{2,1,0:T(8,128)(2,1)} %broadcast_in_dim.52), calls=%async_computation.2 | async-start | bytes 3145728 | tf_op jit(solution)/shard_map/all_to_all | solution.py:13
  100.0 12.1 %all-to-all-done.2 = bf16[4,128,1536]{2,1,0:T(8,128)(2,1)} async-done(((bf16[4,128,1536]{2,1,0:T(8,128)(2,1)}), bf16[4,128,1536]{2,1,0:T(8,128)(2,1)}, u32[]{:S(2)}, u32[]{:S(2)}) %all-to-all-start.2) | async-done | bytes 1572896 | tf_op jit(solution)/shard_map/all_to_all | solution.py:13
  112.2 2.6 %fusion.8 = bf16[512,896]{1,0:T(8,128)(2,1)S(1)} fusion(bf16[896,1536]{0,1:T(8,128)(2,1)S(1)} %bitcast.77, bf16[512,1536]{1,0:T(8,128)(2,1)} %bitcast.22), kind=kOutput, calls=%fused_computation.13 | convolution fusion | flops 939982848 | bytes 3801088 | tf_op jit(solution)/shard_map/dot_general | solution.py:99
  114.8 1.7 convolution_convert_fusion.1
  116.5 2.4 %convolution_convert_fusion = bf16[896,1024]{1,0:T(8,128)(2,1)S(1)} fusion(bf16[512,1536]{1,0:T(8,128)(2,1)} %bitcast.22, bf16[512,1800]{1,0:T(8,128)(2,1)S(1)} %bitcast.82), kind=kOutput, calls=%fused_computation.6 | convolution fusion | flops 940441600 | bytes 3801088 | tf_op jit(solution)/shard_map/dot_general | solution.py:106
  120.0 5.9 %collective-permute-start.3 = (bf16[4,32,1024]{2,1,0:T(8,128)(2,1)}, bf16[4,32,1024]{2,1,0:T(8,128)(2,1)S(1)}, u32[]{:S(2)}, u32[]{:S(2)}) collective-permute-start(bf16[4,32,1024]{2,1,0:T(8,128)(2,1)} %get-tuple-element.20), channel_id=1, source_target_pairs={{4,0},{8,4},{12,8},{16,12},{20,16},{24,20},{28,24},{32,28},{36,32}... | collective-permute-start | bytes 786440 | tf_op jit(solution)/shard_map/ppermute | solution.py:36
  125.9 1.9 collective-permute-start.2
  128.0 2.3 %reshape.114 = bf16[896,3,4,128]{3,2,1,0:T(4,128)(2,1)} reshape(bf16[896,1536]{1,0:T(8,128)(2,1)S(1)} %pad_maximum_fusion) | data formatting | bytes 5505024 | tf_op jit(solution)/shard_map/reshape | solution.py:113
  130.3 3.8 %copy.86 = bf16[896,3,4,128]{3,0,1,2:T(8,128)(2,1)} copy(bf16[896,3,4,128]{3,2,1,0:T(4,128)(2,1)} %reshape.114) | data formatting | bytes 5505024 | tf_op jit(solution)/shard_map/reshape | solution.py:113
  135.6 29.0 %all_to_all.25 = bf16[8,32,1024]{2,1,0:T(8,128)(2,1)S(1)} all-to-all(bf16[8,32,1024]{2,1,0:T(8,128)(2,1)S(1)} %add_convert_fusion), channel_id=1, replica_groups={{0,8,16,24,32,40,48,56},{4,12,20,28,36,44,52,60},{64,72,80,88,96,104,11..., dimensions={0} | all-to-all | bytes 1048576 | tf_op jit(solution)/shard_map/all_to_all | solution.py:13
  165.3 3.3 %all-to-all-start.4 = ((bf16[4,8,896]{2,1,0:T(8,128)(2,1)}), bf16[4,8,896]{2,1,0:T(8,128)(2,1)S(1)}, u32[]{:S(2)}, u32[]{:S(2)}) async-start(bf16[4,8,896]{2,1,0:T(8,128)(2,1)} %fusion.24), calls=%async_computation.4 | async-start | bytes 114688 | tf_op jit(solution)/shard_map/all_to_all | solution.py:13
  168.6 4.7 %all-to-all-done.4 = bf16[4,8,896]{2,1,0:T(8,128)(2,1)S(1)} async-done(((bf16[4,8,896]{2,1,0:T(8,128)(2,1)}), bf16[4,8,896]{2,1,0:T(8,128)(2,1)S(1)}, u32[]{:S(2)}, u32[]{:S(2)}) %all-to-all-start.4) | async-done | bytes 57376 | tf_op jit(solution)/shard_map/all_to_all | solution.py:13
  173.3 14.6 %collective-permute-start.4 = (bf16[1,8,3584]{2,1,0:T(8,128)(2,1)S(1)}, bf16[1,8,3584]{2,1,0:T(8,128)(2,1)S(1)}, u32[]{:S(2)}, u32[]{:S(2)}) collective-permute-start(bf16[1,8,3584]{2,1,0:T(8,128)(2,1)S(1)} %bitcast.90), channel_id=1, source_target_pairs={{0,256},{256,0},{1,257},{257,1},{2,258},{258,2},{3,259},{259,3},{4... | collective-permute-start | bytes 172040 | tf_op jit(solution)/shard_map/ppermute | solution.py:126
  (73 shorter events, 16.1 us)
Async XLA Ops:
  7.2 2.2 %copy-start.7 = (bf16[1,8,3584]{2,1,0:T(8,128)(2,1)S(1)}, bf16[1,8,3584]{2,1,0:T(8,128)(2,1)}, u32[]{:S(2)}) copy-start(bf16[1,8,3584]{2,1,0:T(8,128)(2,1)} %param.8) | copy-start | bytes 172036
  7.2 2.2 %copy-start.8 = (bf16[1,8,3584]{2,1,0:T(8,128)(2,1)S(1)}, bf16[1,8,3584]{2,1,0:T(8,128)(2,1)}, u32[]{:S(2)}) copy-start(bf16[1,8,3584]{2,1,0:T(8,128)(2,1)} %param.7) | copy-start | bytes 172036
  7.2 7.7 %copy-start.11 = (bf16[1,8,4]{1,2,0:T(4,128)(2,1)S(1)}, bf16[1,8,4]{1,2,0:T(4,128)(2,1)}, u32[]{:S(2)}) copy-start(bf16[1,8,4]{1,2,0:T(4,128)(2,1)} %param.10) | copy-start | bytes 196
  7.2 7.7 %copy-start.9 = (s32[1,8,4]{1,2,0:T(4,128)S(1)}, s32[1,8,4]{1,2,0:T(4,128)}, u32[]{:S(2)}) copy-start(s32[1,8,4]{1,2,0:T(4,128)} %param.9) | copy-start | bytes 388
  7.2 56.0 %all-gather.4.cloned.1.call-start = ((), (), s32[]{:S(2)}) async-start(), calls=%async_computation.7 | async-start | bytes 3440640 | tf_op jit(solution)/shard_map/all_gather | solution.py:40
  10.1 9.6 %all-to-all-start = ((bf16[4,16,896]{2,1,0:T(8,128)(2,1)}), bf16[4,16,896]{2,1,0:T(8,128)(2,1)S(1)}, u32[]{:S(2)}, u32[]{:S(2)}) async-start(bf16[4,16,896]{2,1,0:T(8,128)(2,1)} %maximum_bitcast_fusion.1), calls=%async_computation | async-start | bytes 229376 | tf_op jit(solution)/shard_map/all_to_all | solution.py:13
  56.6 11.1 %collective-permute-start = (bf16[4,32,1800]{2,1,0:T(8,128)(2,1)S(1)}, bf16[4,32,1800]{2,1,0:T(8,128)(2,1)S(1)}, u32[]{:S(2)}, u32[]{:S(2)}) collective-permute-start(bf16[4,32,1800]{2,1,0:T(8,128)(2,1)S(1)} %bitcast.86), channel_id=1, source_target_pairs={{0,4},{4,8},{8,12},{12,16},{16,20},{20,24},{24,28},{28,32},{32,36}... | collective-permute-start | bytes 1382408 | tf_op jit(solution)/shard_map/ppermute | solution.py:35
  58.6 10.3 %collective-permute-start.1 = (bf16[4,32,1800]{2,1,0:T(8,128)(2,1)S(1)}, bf16[4,32,1800]{2,1,0:T(8,128)(2,1)S(1)}, u32[]{:S(2)}, u32[]{:S(2)}) collective-permute-start(bf16[4,32,1800]{2,1,0:T(8,128)(2,1)S(1)} %bitcast.85), channel_id=1, source_target_pairs={{4,0},{8,4},{12,8},{16,12},{20,16},{24,20},{28,24},{32,28},{36,32}... | collective-permute-start | bytes 1382408 | tf_op jit(solution)/shard_map/ppermute | solution.py:36
  68.9 0.8 copy-start.6
  71.0 2.5 %copy-start.2 = (bf16[896,3,4,128]{0,3,2,1:T(8,128)(2,1)S(1)}, bf16[896,3,4,128]{0,3,2,1:T(8,128)(2,1)}, u32[]{:S(2)}) copy-start(bf16[896,3,4,128]{0,3,2,1:T(8,128)(2,1)} %copy.61) | copy-start | bytes 8257540
  71.1 4.3 %copy-start.4 = (bf16[4,16,8,1800]{3,2,1,0:T(8,128)(2,1)}, bf16[4,16,8,1800]{3,2,1,0:T(8,128)(2,1)S(1)}, u32[]{:S(2)}) copy-start(bf16[4,16,8,1800]{3,2,1,0:T(8,128)(2,1)S(1)} %copy.62) | copy-start | bytes 5529604
  76.8 16.2 %all-to-all-start.1 = ((bf16[4,128,1536]{2,1,0:T(8,128)(2,1)}), bf16[4,128,1536]{2,1,0:T(8,128)(2,1)S(1)}, u32[]{:S(2)}, u32[]{:S(2)}) async-start(bf16[4,128,1536]{2,1,0:T(8,128)(2,1)} %bitcast.73), calls=%async_computation.1 | async-start | bytes 3145728 | tf_op jit(solution)/shard_map/all_to_all | solution.py:13
  94.9 17.2 %copy-start.3 = (bf16[896,3,4,128]{0,3,2,1:T(8,128)(2,1)S(1)}, bf16[896,3,4,128]{0,3,2,1:T(8,128)(2,1)}, u32[]{:S(2)}) copy-start(bf16[896,3,4,128]{0,3,2,1:T(8,128)(2,1)} %copy.61) | copy-start | bytes 8257540
  94.9 17.2 %all-to-all-start.2 = ((bf16[4,128,1536]{2,1,0:T(8,128)(2,1)}), bf16[4,128,1536]{2,1,0:T(8,128)(2,1)}, u32[]{:S(2)}, u32[]{:S(2)}) async-start(bf16[4,128,1536]{2,1,0:T(8,128)(2,1)} %broadcast_in_dim.52), calls=%async_computation.2 | async-start | bytes 3145728 | tf_op jit(solution)/shard_map/all_to_all | solution.py:13
  99.6 89.2 %reduce-scatter.2.cloned.1.call-start = ((), (), s32[]{:S(2)}) async-start(), calls=%async_computation.6 | async-start | bytes 3440640 | tf_op jit(solution)/shard_map/reduce_scatter | solution.py:115
  112.2 2.6 %copy-start.5 = (bf16[4,16,8,1800]{3,2,1,0:T(8,128)(2,1)S(1)}, bf16[4,16,8,1800]{3,2,1,0:T(8,128)(2,1)}, u32[]{:S(2)}) copy-start(bf16[4,16,8,1800]{3,2,1,0:T(8,128)(2,1)} %copy-done.4) | copy-start | bytes 5529604
  119.1 6.7 %copy-start = (bf16[16,32,1024]{2,1,0:T(8,128)(2,1)}, bf16[16,32,1024]{2,1,0:T(8,128)(2,1)S(1)}, u32[]{:S(2)}) copy-start(bf16[16,32,1024]{2,1,0:T(8,128)(2,1)S(1)} %fusion.11) | copy-start | bytes 3145732
  120.0 14.2 %collective-permute-start.3 = (bf16[4,32,1024]{2,1,0:T(8,128)(2,1)}, bf16[4,32,1024]{2,1,0:T(8,128)(2,1)S(1)}, u32[]{:S(2)}, u32[]{:S(2)}) collective-permute-start(bf16[4,32,1024]{2,1,0:T(8,128)(2,1)} %get-tuple-element.20), channel_id=1, source_target_pairs={{4,0},{8,4},{12,8},{16,12},{20,16},{24,20},{28,24},{32,28},{36,32}... | collective-permute-start | bytes 786440 | tf_op jit(solution)/shard_map/ppermute | solution.py:36
  125.9 8.3 %collective-permute-start.2 = (bf16[4,32,1024]{2,1,0:T(8,128)(2,1)S(1)}, bf16[4,32,1024]{2,1,0:T(8,128)(2,1)S(1)}, u32[]{:S(2)}, u32[]{:S(2)}) collective-permute-start(bf16[4,32,1024]{2,1,0:T(8,128)(2,1)S(1)} %get-tuple-element.21), channel_id=1, source_target_pairs={{0,4},{4,8},{8,12},{12,16},{16,20},{20,24},{24,28},{28,32},{32,36}... | collective-permute-start | bytes 786440 | tf_op jit(solution)/shard_map/ppermute | solution.py:35
  134.2 1.2 copy-start.1
  135.4 52.5 %copy-start.10 = (s32[1,8,4]{1,2,0:T(4,128)S(1)}, s32[1,8,4]{1,2,0:T(4,128)}, u32[]{:S(2)}) copy-start(s32[1,8,4]{1,2,0:T(4,128)} %param.9) | copy-start | bytes 388
  165.3 8.0 %all-to-all-start.4 = ((bf16[4,8,896]{2,1,0:T(8,128)(2,1)}), bf16[4,8,896]{2,1,0:T(8,128)(2,1)S(1)}, u32[]{:S(2)}, u32[]{:S(2)}) async-start(bf16[4,8,896]{2,1,0:T(8,128)(2,1)} %fusion.24), calls=%async_computation.4 | async-start | bytes 114688 | tf_op jit(solution)/shard_map/all_to_all | solution.py:13
  173.3 15.4 %collective-permute-start.4 = (bf16[1,8,3584]{2,1,0:T(8,128)(2,1)S(1)}, bf16[1,8,3584]{2,1,0:T(8,128)(2,1)S(1)}, u32[]{:S(2)}, u32[]{:S(2)}) collective-permute-start(bf16[1,8,3584]{2,1,0:T(8,128)(2,1)S(1)} %bitcast.90), channel_id=1, source_target_pairs={{0,256},{256,0},{1,257},{257,1},{2,258},{258,2},{3,259},{259,3},{4... | collective-permute-start | bytes 172040 | tf_op jit(solution)/shard_map/ppermute | solution.py:126
Sparse Core Ops, SparseCore 0:
  10.1 49.2 all-gather.3
  134.4 51.6 reduce-scatter.1

commit v3 on v2

v3 whole, which is shorter than its diff:
```python
import functools

import jax
import jax.numpy as jnp
from jax import lax
from jax.experimental import pallas as pl
from jax.experimental.pallas import tpu as pltpu
from jax.sharding import PartitionSpec as P

BF16 = jnp.bfloat16
F32 = jnp.float32
LANES = 128
contract_first = (((0,), (0,)), ((), ()))
contract_last = (((1,), (1,)), ((), ()))


def exchange(blocks, axis, groups=None):
    return lax.all_to_all(blocks, axis, 0, 0, axis_index_groups=groups, tiled=True)


def whole(shape):
    return pl.BlockSpec(shape, lambda y: (0,) * len(shape))


def params():
    return pltpu.CompilerParams(
        dimension_semantics=("arbitrary",), vmem_limit_bytes=20 * 1024 * 1024
    )


def gather_rows(n_x, cols, own, low, high, outs):
    count = own.shape[0]
    quarter = low.shape[0]
    for x in range(n_x):
        base = 2 * x * count
        for part, out in enumerate(outs):
            lanes = slice((2 * x + part) * cols, (2 * x + part + 1) * cols)
            out[base : base + count, :] = own[:, lanes]
            out[base + count : base + count + quarter, :] = low[:, lanes]
            out[base + count + quarter : base + 2 * count, :] = high[:, lanes]


def forward_kernel(n_x, cols, own, low, high, weights, partial, x_rows, g_rows, held, arrived):
    y = pl.program_id(0)
    ff = weights.shape[3]

    def copies(step):
        return [
            pltpu.make_async_copy(
                weights.at[step, k],
                held.at[step, :, k * ff : (k + 1) * ff],
                arrived.at[step, k],
            )
            for k in range(3)
        ]

    @pl.when(y == 0)
    def _():
        for step in range(held.shape[0]):
            for copy in copies(step):
                copy.start()
        gather_rows(n_x, cols, own, low, high, (x_rows, g_rows))

    for copy in copies(y):
        copy.wait()
    first = jnp.dot(x_rows[...], held[y, :, : 2 * ff], preferred_element_type=F32)
    partial[:, : 2 * ff] = first.astype(BF16)
    second = jnp.dot(g_rows[...], held[y, :, 2 * ff :], preferred_element_type=F32)
    partial[:, 2 * ff :] = second.astype(BF16)


def forward(own, low, high, weights, n_x):
    n_y, three, cols, ff = weights.shape
    rows = 2 * n_x * own.shape[0]
    return pl.pallas_call(
        functools.partial(forward_kernel, n_x, cols),
        grid=(n_y,),
        in_specs=[
            whole(own.shape),
            whole(low.shape),
            whole(high.shape),
            pl.BlockSpec(memory_space=pltpu.HBM),
        ],
        out_specs=pl.BlockSpec((rows, three * ff), lambda y: (0, y)),
        out_shape=pltpu.HBM((rows, n_y * three * ff), BF16),
        scratch_shapes=[
            pltpu.VMEM((rows, cols), BF16),
            pltpu.VMEM((rows, cols), BF16),
            pltpu.VMEM((n_y, cols, three * ff), BF16),
            pltpu.SemaphoreType.DMA((n_y, three)),
        ],
        compiler_params=params(),
        cost_estimate=pl.CostEstimate(
            flops=2 * rows * cols * n_y * three * ff, bytes_accessed=7_000_000, transcendentals=0
        ),
    )(own, low, high, weights)


def hidden_kernel(half, partial, own, low, high, grads, score):
    n_x, rows, total = partial.shape
    ff = total // 3
    y = pl.program_id(0)
    column = 2 * y + half[0]
    dense = jnp.concatenate([own[...], low[...], high[...]], axis=0).astype(F32)
    lane = lax.broadcasted_iota(jnp.int32, dense.shape, 1)
    route = jnp.sum(jnp.where(lane == column, dense, 0.0), axis=1, keepdims=True)
    full = partial[0].astype(F32)
    for x in range(1, n_x):
        full = full + partial[x].astype(F32)
    gate = full[:, :ff]
    up = full[:, ff : 2 * ff]
    down_grad = full[:, 2 * ff :]
    sig = jax.nn.sigmoid(gate)
    act = gate * sig
    hidden = act * up
    total_score = jnp.sum(hidden * down_grad, axis=1, keepdims=True)
    placed = jnp.where(lane == column, total_score, 0.0).astype(BF16)

    @pl.when(y == 0)
    def _():
        score[...] = placed

    @pl.when(y > 0)
    def _():
        score[...] += placed

    hidden_grad = down_grad * route
    gate_grad = (hidden_grad * up * sig * (1.0 + gate * (1.0 - sig))).astype(BF16)
    up_grad = (hidden_grad * act).astype(BF16)
    weighted = (hidden * route).astype(BF16)
    for x in range(n_x):
        grads[x, :, :ff] = gate_grad
        grads[x, :, ff : 2 * ff] = up_grad
        grads[x, :, 2 * ff :] = weighted


def hidden_part(half, partial, own, low, high, n_y):
    n_x, rows, total = partial.shape
    lanes = own.shape[1] // LANES - 1
    block = pl.BlockSpec((n_x, rows, total // n_y), lambda y: (0, 0, y))
    tails = [pl.BlockSpec((p.shape[0], LANES), lambda y: (0, lanes)) for p in (own, low, high)]
    return pl.pallas_call(
        hidden_kernel,
        grid=(n_y,),
        in_specs=[pl.BlockSpec(memory_space=pltpu.SMEM), block] + tails,
        out_specs=[block, whole((rows, LANES))],
        out_shape=[
            pltpu.HBM(partial.shape, BF16),
            jax.ShapeDtypeStruct((rows, LANES), BF16),
        ],
        compiler_params=params(),
        cost_estimate=pl.CostEstimate(
            flops=20 * rows * total, bytes_accessed=4 * n_x * rows * total, transcendentals=rows * total // 3
        ),
    )(half, partial, own, low, high)


def input_kernel(n_x, grads, weights, score, mine, low, high, total, held, arrived):
    n_y = weights.shape[0]
    ff = weights.shape[3]
    cols = weights.shape[2]
    rows = score.shape[0]
    copies = []
    for y in range(n_y):
        for k in range(2):
            copies.append(
                pltpu.make_async_copy(
                    weights.at[y, k], held.at[y, :, k * ff : (k + 1) * ff], arrived.at[y, k]
                )
            )
    for copy in copies:
        copy.start()
    for y in range(n_y):
        copies[2 * y].wait()
        copies[2 * y + 1].wait()
        product = lax.dot_general(
            grads[:, 3 * y * ff : (3 * y + 2) * ff],
            held[y],
            contract_last,
            preferred_element_type=F32,
        )
        if y == 0:
            total[...] = product
        else:
            total[...] += product
    first = 0
    for out in (mine, low, high):
        count = out.shape[0]
        for x in range(n_x):
            part = total[x * rows + first : x * rows + first + count, :]
            out[:, x * cols : (x + 1) * cols] = part.astype(BF16)
        out[:, n_x * cols :] = score[first : first + count, :]
        first += count


def input_grad(grads, weights, score, n_x):
    n_y, three, cols, ff = weights.shape
    rows = score.shape[0]
    width = n_x * cols + score.shape[1]
    counts = (rows // 2, rows // 4, rows // 4)
    vmem = pl.BlockSpec(memory_space=pltpu.VMEM)
    return pl.pallas_call(
        functools.partial(input_kernel, n_x),
        in_specs=[vmem, pl.BlockSpec(memory_space=pltpu.HBM), vmem],
        out_specs=[vmem] * 3,
        out_shape=[jax.ShapeDtypeStruct((count, width), BF16) for count in counts],
        scratch_shapes=[
            pltpu.VMEM((n_x * rows, cols), F32),
            pltpu.VMEM((n_y, cols, 2 * ff), BF16),
            pltpu.SemaphoreType.DMA((n_y, 2)),
        ],
        compiler_params=pltpu.CompilerParams(vmem_limit_bytes=20 * 1024 * 1024),
        cost_estimate=pl.CostEstimate(
            flops=4 * n_x * rows * cols * n_y * ff, bytes_accessed=6_000_000, transcendentals=0
        ),
    )(grads, weights, score)


def weight_kernel(n_x, cols, own, low, high, grads, out, x_rows, g_rows):
    ff = out.shape[3]

    @pl.when(pl.program_id(0) == 0)
    def _():
        gather_rows(n_x, cols, own, low, high, (x_rows, g_rows))

    product = lax.dot_general(
        x_rows[...], grads[:, : 2 * ff], contract_first, preferred_element_type=F32
    )
    out[0, 0] = product[:, :ff].astype(BF16)
    out[0, 1] = product[:, ff:].astype(BF16)
    product = lax.dot_general(
        g_rows[...], grads[:, 2 * ff :], contract_first, preferred_element_type=F32
    )
    out[0, 2] = product.astype(BF16)


def weight_grad(own, low, high, grads, n_x, n_y, cols):
    rows, total = grads.shape
    ff = total // (3 * n_y)
    return pl.pallas_call(
        functools.partial(weight_kernel, n_x, cols),
        grid=(n_y,),
        in_specs=[
            whole(own.shape),
            whole(low.shape),
            whole(high.shape),
            pl.BlockSpec((rows, 3 * ff), lambda y: (0, y)),
        ],
        out_specs=pl.BlockSpec((1, 3, cols, ff), lambda y: (y, 0, 0, 0)),
        out_shape=pltpu.HBM((n_y, 3, cols, ff), BF16),
        scratch_shapes=[pltpu.VMEM((rows, cols), BF16), pltpu.VMEM((rows, cols), BF16)],
        compiler_params=params(),
        cost_estimate=pl.CostEstimate(
            flops=6 * rows * cols * n_y * ff, bytes_accessed=7_000_000, transcendentals=0
        ),
    )(own, low, high, grads)


def body(tokens, grad_out, routes, combine, w_gate, w_up, w_down):
    tok, width = tokens.shape[1:]
    experts = 8
    n_x = lax.axis_size("dp")
    n_e = lax.axis_size("expert")
    n_z = 2 * (n_e // experts)
    n_y = n_e // n_z
    half = n_z // 2
    cols = width // n_x
    along_y = [[y * n_z + z for y in range(n_y)] for z in range(n_z)]
    same_parity = [[y * n_z + 2 * i + p for i in range(half)] for y in range(n_y) for p in range(2)]
    up_z = [(y * n_z + z, y * n_z + (z + 1) % n_z) for y in range(n_y) for z in range(n_z)]
    down_z = [(b, a) for a, b in up_z]
    upper_half = (lax.axis_index("expert") % n_z >= half).astype(jnp.int32)
    own_rows = half * tok
    all_rows = n_z * tok

    both = jnp.concatenate([tokens[0], grad_out[0]], axis=0).reshape(2 * tok, n_x, cols)
    both = both.transpose(1, 0, 2)
    both, w_gate, w_up, w_down = lax.optimization_barrier((both, w_gate, w_up, w_down))

    weights = jnp.stack([w_gate[0], w_up[0], w_down[0]])
    weights = lax.all_gather(weights, "expert", axis_index_groups=along_y)

    both = exchange(both, "dp")
    chosen = routes[0][:, :, None] == jnp.arange(experts, dtype=jnp.int32)
    dense = jnp.sum(jnp.where(chosen, combine[0].astype(F32)[:, :, None], 0.0), axis=1)
    dense = jnp.pad(dense.astype(BF16), ((0, 0), (0, LANES - experts)))
    pieces = [both[x, p * tok : (p + 1) * tok] for x in range(n_x) for p in range(2)]
    line = jnp.concatenate(pieces + [dense], axis=1)

    own = lax.all_gather(line, "expert", axis_index_groups=same_parity, tiled=True)
    low = lax.ppermute(own[: own_rows // 2], "expert", up_z)
    high = lax.ppermute(own[own_rows // 2 :], "expert", down_z)
    partial = forward(own, low, high, weights, n_x)
    partial = exchange(partial.reshape(n_x, all_rows, -1), "dp")
    grads, score = hidden_part(upper_half[None], partial, own, low, high, n_y)
    grads = exchange(grads, "dp").reshape(n_x * all_rows, -1)

    total = weight_grad(own, low, high, grads, n_x, n_y, cols)
    total, grads = lax.optimization_barrier((total, grads))
    total = lax.psum_scatter(total, "expert", scatter_dimension=0, axis_index_groups=along_y)

    mine, send_up, send_down = input_grad(grads, weights, score, n_x)
    from_below = lax.ppermute(send_up, "expert", up_z)
    from_above = lax.ppermute(send_down, "expert", down_z)
    back = mine.astype(F32) + jnp.concatenate([from_below, from_above], axis=0).astype(F32)
    back = exchange(back.astype(BF16).reshape(half, tok, -1), "expert", same_parity)
    back = jnp.sum(back.astype(F32), axis=0)
    back, total = lax.optimization_barrier((back, total))
    grads = [total[k : k + 1].astype(F32) for k in range(3)]
    score = back[:, width : width + experts]
    grad_combine = jnp.sum(jnp.where(chosen, score[:, None, :], 0.0), axis=2)[None]
    passed = jnp.stack([back[:, x * cols : (x + 1) * cols] for x in range(n_x)])
    passed = exchange(passed.astype(BF16), "dp")
    passed = jnp.concatenate([passed[x] for x in range(n_x)], axis=1)[None]
    passed, grads = lax.optimization_barrier((passed, grads))
    sections = lax.axis_size("pipe")
    passed = lax.ppermute(passed, "pipe", [(s, (s - 1) % sections) for s in range(sections)])
    return passed, grad_combine, *grads


def solution(mesh):
    row_spec = P("pipe", ("expert", "dp"), None)
    weight_spec = P("pipe", "dp", "expert")
    in_specs = (row_spec,) * 4 + (weight_spec,) * 3
    out_specs = (row_spec,) * 2 + (weight_spec,) * 3
    return jax.shard_map(body, mesh=mesh, in_specs=in_specs, out_specs=out_specs, check_vma=False)
```

time: 200 us -> 196 us (0.980)
  blocking collectives: 65.9 us -> 92.3 us
  local copies, waits for them, and re-layouts: 20.3 us -> 4.33 us
  Pallas kernels: 0 us -> 12.8 us
  starting transfers between devices: 45.2 us -> 35.8 us
  matrix products: 8.73 us -> 0 us
  waiting for transfers between devices: 35.2 us -> 28.7 us
    all_to_all x1 -> x2, blocking collectives: 29 us -> 56.7 us  [exchange(): lax.all_to_all(blocks, axis, 0, 0, axis_index_groups=groups, tiled=True)]
    all_to_all x4 -> x3, waiting for transfers between devices: 33.8 us -> 17.1 us  [exchange(): lax.all_to_all(blocks, axis, 0, 0, axis_index_groups=groups, tiled=True)]
    pallas_call x0 -> x4, Pallas kernels: none -> 12.8 us  [the longest x1 4.34 us: forward(): pl.pallas_call(functools.partial(forward_kernel, n_x, cols), grid=(n_y,),...]
    ppermute x4, waiting for transfers between devices: 1.23 us -> 11.4 us  [the longest x1 4.87 us: body(): high = lax.ppermute(own[own_rows // 2:], 'expert', down_z)]
    dot_general x5 -> x0, matrix products: 8.73 us -> none  [the longest x1 2.61 us: body(): lax.dot_general(grads[:, :2 * wide], weights[:, :2 * wide], contract_last...]
    reshape x5 -> x0, local copies, waits for them, and re-layouts: 6.86 us -> none  [the longest x2 6.14 us: body(): total = total.reshape(cols, 3, n_y, ff).transpose(2, 1, 0, 3)]
    ppermute x1, starting transfers between devices: 14.6 us -> 9.49 us  [body(): lax.ppermute(passed, 'pipe', [(s, (s - 1) % sections) for s in range(sect...]
    transpose x2 -> x0, local copies, waits for them, and re-layouts: 4.7 us -> none  [the longest x1 4.55 us: body(): weights = weights.transpose(2, 1, 0, 3).reshape(cols, 3 * wide)]
  transfers between devices with their start and end apart: 11 -> 10, of which waited for: 7 -> 8; matrix products, arithmetic and copies ran while one was open for 7% -> 3% of each run, Pallas kernels for 0% -> 1%
where the time goes in v3:
time: 196 us
  blocking collectives  92.3 us (47%)
  starting transfers between devices  35.8 us (18%)
  waiting for transfers between devices  28.7 us (15%)
  between operations  14.2 us (7%)
  Pallas kernels  12.8 us (7%)
  other arithmetic  7.5 us (4%)
  local copies, waits for them, and re-layouts  4.33 us (2%)
    all_to_all x2, blocking collectives, exchange(): lax.all_to_all(blocks, axis, 0, 0, axis_index_groups=groups, tiled=True)  56.7 us
    all_gather x1, blocking collectives, body(): lax.all_gather(line, 'expert', axis_index_groups=same_parity, tiled=True)  35.6 us
    all_to_all x3, waiting for transfers between devices, exchange(): lax.all_to_all(blocks, axis, 0, 0, axis_index_groups=groups, tiled=True)  17.1 us
    all_to_all x3, starting transfers between devices, exchange(): lax.all_to_all(blocks, axis, 0, 0, axis_index_groups=groups, tiled=True)  11.7 us
    ppermute x1, starting transfers between devices, body(): lax.ppermute(passed, 'pipe', [(s, (s - 1) % sections) for s in range(sect...  9.49 us
    ppermute x1, starting transfers between devices, body(): from_above = lax.ppermute(send_down, 'expert', down_z)  7.18 us
    ppermute x1, waiting for transfers between devices, body(): high = lax.ppermute(own[own_rows // 2:], 'expert', down_z)  4.87 us
    pallas_call x1, Pallas kernels, forward(): pl.pallas_call(functools.partial(forward_kernel, n_x, cols), grid=(n_y,),...  4.34 us
  transfers between devices with their start and end apart: 10, of which 8 were waited for; matrix products, arithmetic and copies ran while one was open for 3% of the time, Pallas kernels for 1%

profile of v3, /device:TPU:1, one launch (start us, length us, event | category | flops | bytes accessed | tf_op | source)
XLA Modules:
  0.0 195.6 jit_solution(8388396349154536996)
XLA Ops:
  8.7 4.8 %all-to-all-start = ((bf16[4,16,896]{2,1,0:T(8,128)(2,1)}), bf16[4,16,896]{2,1,0:T(8,128)(2,1)S(1)}, u32[]{:S(2)}, u32[]{:S(2)}) async-start(bf16[4,16,896]{2,1,0:T(8,128)(2,1)} %maximum_bitcast_fusion), calls=%async_computation | async-start | bytes 229376 | tf_op jit(solution)/shard_map/all_to_all | solution.py:18
  13.5 2.1 %pad_maximum_fusion = bf16[3,896,128]{2,1,0:T(8,128)(2,1)} fusion(bf16[1,896,128]{2,1,0:T(8,128)(2,1)} %param.13, bf16[1,896,128]{2,1,0:T(8,128)(2,1)} %param.12, bf16[1,896,128]{2,1,0:T(8,128)(2,1)} %param.11), kind=kLoop, calls=%fused_computation.2 | loop fusion | flops 688128 | bytes 1376256 | tf_op jit(solution)/shard_map/stack | solution.py:280
  15.8 2.5 %all-to-all-done = bf16[4,16,896]{2,1,0:T(8,128)(2,1)S(1)} async-done(((bf16[4,16,896]{2,1,0:T(8,128)(2,1)}), bf16[4,16,896]{2,1,0:T(8,128)(2,1)S(1)}, u32[]{:S(2)}, u32[]{:S(2)}) %all-to-all-start) | async-done | bytes 114720 | tf_op jit(solution)/shard_map/all_to_all | solution.py:18
  18.4 35.6 %all_gather.9.own = bf16[64,7296]{1,0:T(8,128)(2,1)S(1)} all-gather(bf16[8,7296]{1,0:T(8,128)(2,1)S(1)} %constant_dynamic-update-slice_fusion), channel_id=1, replica_groups={{0,8,16,24,32,40,48,56},{4,12,20,28,36,44,52,60},{64,72,80,88,96,104,11..., dimensions={0}, use_global_device_ids=true | all-gather | bytes 1050624 | tf_op jit(solution)/shard_map/all_gather | solution.py:290
  54.0 3.1 %collective-permute-start.1 = (bf16[32,7296]{1,0:T(8,128)(2,1)S(1)}, bf16[32,7296]{1,0:T(8,128)(2,1)S(1)}, u32[]{:S(2)}, u32[]{:S(2)}) collective-permute-start(bf16[32,7296]{1,0:T(8,128)(2,1)S(1)} %get-tuple-element.39), channel_id=1, source_target_pairs={{4,0},{8,4},{12,8},{16,12},{20,16},{24,20},{28,24},{32,28},{36,32}... | collective-permute-start | bytes 1400840 | tf_op jit(solution)/shard_map/ppermute | solution.py:292
  57.1 2.1 %collective-permute-start = (bf16[32,7296]{1,0:T(8,128)(2,1)S(1)}, bf16[32,7296]{1,0:T(8,128)(2,1)S(1)}, u32[]{:S(2)}, u32[]{:S(2)}) collective-permute-start(bf16[32,7296]{1,0:T(8,128)(2,1)S(1)} %get-tuple-element.40), channel_id=1, source_target_pairs={{0,4},{4,8},{8,12},{12,16},{16,20},{20,24},{24,28},{28,32},{32,36}... | collective-permute-start | bytes 1400840 | tf_op jit(solution)/shard_map/ppermute | solution.py:291
  59.3 4.9 %collective-permute-done.1.high = bf16[32,7296]{1,0:T(8,128)(2,1)S(1)} collective-permute-done((bf16[32,7296]{1,0:T(8,128)(2,1)S(1)}, bf16[32,7296]{1,0:T(8,128)(2,1)S(1)}, u32[]{:S(2)}, u32[]{:S(2)}) %collective-permute-start.1) | collective-permute-done | bytes 466976 | tf_op jit(solution)/shard_map/ppermute | solution.py:292
  64.2 3.5 %collective-permute-done.low = bf16[32,7296]{1,0:T(8,128)(2,1)S(1)} collective-permute-done((bf16[32,7296]{1,0:T(8,128)(2,1)S(1)}, bf16[32,7296]{1,0:T(8,128)(2,1)S(1)}, u32[]{:S(2)}, u32[]{:S(2)}) %collective-permute-start) | collective-permute-done | bytes 466976 | tf_op jit(solution)/shard_map/ppermute | solution.py:291
  67.7 1.8 copy-done
  69.4 4.3 %shard_map.110 = bf16[512,1536]{1,0:T(8,128)(2,1)} custom-call(bf16[64,7296]{1,0:T(8,128)(2,1)S(1)} %all_gather.9.own, bf16[32,7296]{1,0:T(8,128)(2,1)S(1)} %collective-permute-done.low, bf16[32,7296]{1,0:T(8,128)(2,1)S(1)} %collective-permute-done.1.high, bf16[4,3,896,128]{3,2,1,0:T(8,128)(2,1)S(1)} %bitcast.68), custom_call_target="tpu_custom_call" | custom-call | flops 1409286144 | bytes 7000000 | tf_op jit(solution)/shard_map/pallas_call | solution.py:75
  73.8 3.6 %all-to-all-start.1 = ((bf16[4,128,1536]{2,1,0:T(8,128)(2,1)}), bf16[4,128,1536]{2,1,0:T(8,128)(2,1)S(1)}, u32[]{:S(2)}, u32[]{:S(2)}) async-start(bf16[4,128,1536]{2,1,0:T(8,128)(2,1)} %bitcast.70), calls=%async_computation.1 | async-start | bytes 3145728 | tf_op jit(solution)/shard_map/all_to_all | solution.py:18
  77.4 12.5 %all-to-all-done.1.partial = bf16[4,128,1536]{2,1,0:T(8,128)(2,1)S(1)} async-done(((bf16[4,128,1536]{2,1,0:T(8,128)(2,1)}), bf16[4,128,1536]{2,1,0:T(8,128)(2,1)S(1)}, u32[]{:S(2)}, u32[]{:S(2)}) %all-to-all-start.1) | async-done | bytes 1572896 | tf_op jit(solution)/shard_map/all_to_all | solution.py:18
  89.9 2.4 %shard_map.111 = (bf16[4,128,1536]{2,1,0:T(8,128)(2,1)}, bf16[128,128]{1,0:T(8,128)(2,1)S(1)}) custom-call(s32[1]{0:T(128)} %bitcast.13.half, bf16[4,128,1536]{2,1,0:T(8,128)(2,1)S(1)} %all-to-all-done.1.partial, bf16[64,7296]{1,0:T(8,128)(2,1)S(1)} %all_gather.9.own, bf16[32,7296]{1,0:T(8,128)(2,1)S(1)} %collective-permute-done.low, ...), custom_call_target="tpu_custom_call" | custom-call | flops 3932160 | bytes 3145728 | tf_op jit(solution)/shard_map/pallas_call | solution.py:142
  92.3 16.1 %all_to_all.25 = bf16[4,128,1536]{2,1,0:T(8,128)(2,1)S(1)} all-to-all(bf16[4,128,1536]{2,1,0:T(8,128)(2,1)} %get-tuple-element.26), channel_id=1, replica_groups=mesh['pipe'=2,'expert'=64,'dp'=4] {'dp'}, dimensions={0} | all-to-all | bytes 3145728 | tf_op jit(solution)/shard_map/all_to_all | solution.py:18
  108.4 4.1 %shard_map.112 = bf16[4,3,896,128]{3,2,1,0:T(8,128)(2,1)} custom-call(bf16[64,7296]{1,0:T(8,128)(2,1)S(1)} %all_gather.9.own, bf16[32,7296]{1,0:T(8,128)(2,1)S(1)} %collective-permute-done.low, bf16[32,7296]{1,0:T(8,128)(2,1)S(1)} %collective-permute-done.1.high, bf16[512,1536]{1,0:T(8,128)(2,1)S(1)} %bitcast.66), custom_call_target="tpu_custom_call" | custom-call | flops 1409286144 | bytes 7000000 | tf_op jit(solution)/shard_map/pallas_call | solution.py:240
  112.5 1.8 copy-done.1
  114.3 1.9 shard_map.113
  116.2 2.1 %collective-permute-start.2 = (bf16[32,3712]{1,0:T(8,128)(2,1)S(1)}, bf16[32,3712]{1,0:T(8,128)(2,1)S(1)}, u32[]{:S(2)}, u32[]{:S(2)}) collective-permute-start(bf16[32,3712]{1,0:T(8,128)(2,1)S(1)} %get-tuple-element.30), channel_id=1, source_target_pairs={{0,4},{4,8},{8,12},{12,16},{16,20},{20,24},{24,28},{28,32},{32,36}... | collective-permute-start | bytes 712712 | tf_op jit(solution)/shard_map/ppermute | solution.py:303
  118.4 7.2 %collective-permute-start.3 = (bf16[32,3712]{1,0:T(8,128)(2,1)S(1)}, bf16[32,3712]{1,0:T(8,128)(2,1)S(1)}, u32[]{:S(2)}, u32[]{:S(2)}) collective-permute-start(bf16[32,3712]{1,0:T(8,128)(2,1)S(1)} %get-tuple-element.31), channel_id=1, source_target_pairs={{4,0},{8,4},{12,8},{16,12},{20,16},{24,20},{28,24},{32,28},{36,32}... | collective-permute-start | bytes 712712 | tf_op jit(solution)/shard_map/ppermute | solution.py:304
  128.7 40.6 %all_to_all.26 = bf16[8,8,3712]{2,1,0:T(8,128)(2,1)S(1)} all-to-all(bf16[8,8,3712]{2,1,0:T(8,128)(2,1)S(1)} %fusion), channel_id=1, replica_groups={{0,8,16,24,32,40,48,56},{4,12,20,28,36,44,52,60},{64,72,80,88,96,104,11..., dimensions={0} | all-to-all | bytes 950272 | tf_op jit(solution)/shard_map/all_to_all | solution.py:18
  170.1 3.3 %all-to-all-start.4 = ((bf16[4,8,896]{2,1,0:T(8,128)(2,1)}), bf16[4,8,896]{2,1,0:T(8,128)(2,1)S(1)}, u32[]{:S(2)}, u32[]{:S(2)}) async-start(bf16[4,8,896]{2,1,0:T(8,128)(2,1)} %pad_maximum_fusion.1), calls=%async_computation.5 | async-start | bytes 114688 | tf_op jit(solution)/shard_map/all_to_all | solution.py:18
  173.4 2.3 %slice_convert_fusion = (f32[1,896,128]{2,1,0:T(8,128)}, f32[1,896,128]{2,1,0:T(8,128)}, f32[1,896,128]{2,1,0:T(8,128)}) fusion(bf16[3,896,128]{2,1,0:T(8,128)(2,1)} %bitcast.71), kind=kLoop, calls=%fused_computation.4 | loop fusion | flops 344064 | bytes 2064384 | tf_op jit(solution)/shard_map/convert_element_type | solution.py:309
  175.7 2.1 %all-to-all-done.4 = bf16[4,8,896]{2,1,0:T(8,128)(2,1)S(1)} async-done(((bf16[4,8,896]{2,1,0:T(8,128)(2,1)}), bf16[4,8,896]{2,1,0:T(8,128)(2,1)S(1)}, u32[]{:S(2)}, u32[]{:S(2)}) %all-to-all-start.4) | async-done | bytes 57376 | tf_op jit(solution)/shard_map/all_to_all | solution.py:18
  177.8 9.5 %collective-permute-start.4 = (bf16[1,8,3584]{2,1,0:T(8,128)(2,1)S(1)}, bf16[1,8,3584]{2,1,0:T(8,128)(2,1)S(1)}, u32[]{:S(2)}, u32[]{:S(2)}) collective-permute-start(bf16[1,8,3584]{2,1,0:T(8,128)(2,1)S(1)} %maximum_bitcast_fusion.1), channel_id=1, source_target_pairs={{0,256},{256,0},{1,257},{257,1},{2,258},{258,2},{3,259},{259,3},{4... | collective-permute-start | bytes 172040 | tf_op jit(solution)/shard_map/ppermute | solution.py:317
  (38 shorter events, 7.2 us)
Async XLA Ops:
  7.2 8.5 %copy-start.3 = (bf16[1,8,4]{1,2,0:T(4,128)(2,1)S(1)}, bf16[1,8,4]{1,2,0:T(4,128)(2,1)}, u32[]{:S(2)}) copy-start(bf16[1,8,4]{1,2,0:T(4,128)(2,1)} %param.10) | copy-start | bytes 196
  7.2 8.5 %copy-start.2 = (s32[1,8,4]{1,2,0:T(4,128)S(1)}, s32[1,8,4]{1,2,0:T(4,128)}, u32[]{:S(2)}) copy-start(s32[1,8,4]{1,2,0:T(4,128)} %param.9) | copy-start | bytes 388
  8.7 9.6 %all-to-all-start = ((bf16[4,16,896]{2,1,0:T(8,128)(2,1)}), bf16[4,16,896]{2,1,0:T(8,128)(2,1)S(1)}, u32[]{:S(2)}, u32[]{:S(2)}) async-start(bf16[4,16,896]{2,1,0:T(8,128)(2,1)} %maximum_bitcast_fusion), calls=%async_computation | async-start | bytes 229376 | tf_op jit(solution)/shard_map/all_to_all | solution.py:18
  13.5 54.1 %all-gather.3.cloned.1.call-start = ((), (), s32[]{:S(2)}) async-start(), calls=%async_computation.7 | async-start | bytes 3440640 | tf_op jit(solution)/shard_map/all_gather | solution.py:281
  54.0 10.2 %collective-permute-start.1 = (bf16[32,7296]{1,0:T(8,128)(2,1)S(1)}, bf16[32,7296]{1,0:T(8,128)(2,1)S(1)}, u32[]{:S(2)}, u32[]{:S(2)}) collective-permute-start(bf16[32,7296]{1,0:T(8,128)(2,1)S(1)} %get-tuple-element.39), channel_id=1, source_target_pairs={{4,0},{8,4},{12,8},{16,12},{20,16},{24,20},{28,24},{32,28},{36,32}... | collective-permute-start | bytes 1400840 | tf_op jit(solution)/shard_map/ppermute | solution.py:292
  57.1 10.5 %collective-permute-start = (bf16[32,7296]{1,0:T(8,128)(2,1)S(1)}, bf16[32,7296]{1,0:T(8,128)(2,1)S(1)}, u32[]{:S(2)}, u32[]{:S(2)}) collective-permute-start(bf16[32,7296]{1,0:T(8,128)(2,1)S(1)} %get-tuple-element.40), channel_id=1, source_target_pairs={{0,4},{4,8},{8,12},{12,16},{16,20},{20,24},{24,28},{28,32},{32,36}... | collective-permute-start | bytes 1400840 | tf_op jit(solution)/shard_map/ppermute | solution.py:291
  67.7 1.8 copy-start
  73.8 16.1 %all-to-all-start.1 = ((bf16[4,128,1536]{2,1,0:T(8,128)(2,1)}), bf16[4,128,1536]{2,1,0:T(8,128)(2,1)S(1)}, u32[]{:S(2)}, u32[]{:S(2)}) async-start(bf16[4,128,1536]{2,1,0:T(8,128)(2,1)} %bitcast.70), calls=%async_computation.1 | async-start | bytes 3145728 | tf_op jit(solution)/shard_map/all_to_all | solution.py:18
  77.4 92.1 %reduce-scatter.2.cloned.1.call-start = ((), (), s32[]{:S(2)}) async-start(), calls=%async_computation.6 | async-start | bytes 3440640 | tf_op jit(solution)/shard_map/reduce_scatter | solution.py:300
  112.5 1.8 copy-start.1
  116.2 10.9 %collective-permute-start.2 = (bf16[32,3712]{1,0:T(8,128)(2,1)S(1)}, bf16[32,3712]{1,0:T(8,128)(2,1)S(1)}, u32[]{:S(2)}, u32[]{:S(2)}) collective-permute-start(bf16[32,3712]{1,0:T(8,128)(2,1)S(1)} %get-tuple-element.30), channel_id=1, source_target_pairs={{0,4},{4,8},{8,12},{12,16},{16,20},{20,24},{24,28},{28,32},{32,36}... | collective-permute-start | bytes 712712 | tf_op jit(solution)/shard_map/ppermute | solution.py:303
  118.4 10.2 %collective-permute-start.3 = (bf16[32,3712]{1,0:T(8,128)(2,1)S(1)}, bf16[32,3712]{1,0:T(8,128)(2,1)S(1)}, u32[]{:S(2)}, u32[]{:S(2)}) collective-permute-start(bf16[32,3712]{1,0:T(8,128)(2,1)S(1)} %get-tuple-element.31), channel_id=1, source_target_pairs={{4,0},{8,4},{12,8},{16,12},{20,16},{24,20},{28,24},{32,28},{36,32}... | collective-permute-start | bytes 712712 | tf_op jit(solution)/shard_map/ppermute | solution.py:304
  170.1 7.7 %all-to-all-start.4 = ((bf16[4,8,896]{2,1,0:T(8,128)(2,1)}), bf16[4,8,896]{2,1,0:T(8,128)(2,1)S(1)}, u32[]{:S(2)}, u32[]{:S(2)}) async-start(bf16[4,8,896]{2,1,0:T(8,128)(2,1)} %pad_maximum_fusion.1), calls=%async_computation.5 | async-start | bytes 114688 | tf_op jit(solution)/shard_map/all_to_all | solution.py:18
  177.8 10.4 %collective-permute-start.4 = (bf16[1,8,3584]{2,1,0:T(8,128)(2,1)S(1)}, bf16[1,8,3584]{2,1,0:T(8,128)(2,1)S(1)}, u32[]{:S(2)}, u32[]{:S(2)}) collective-permute-start(bf16[1,8,3584]{2,1,0:T(8,128)(2,1)S(1)} %maximum_bitcast_fusion.1), channel_id=1, source_target_pairs={{0,256},{256,0},{1,257},{257,1},{2,258},{258,2},{3,259},{259,3},{4... | collective-permute-start | bytes 172040 | tf_op jit(solution)/shard_map/ppermute | solution.py:317
Sparse Core Ops, SparseCore 0:
  16.5 49.2 all-gather.2
  112.6 51.0 reduce-scatter.1

commit v4 on v3

--- a/solution.py
+++ b/solution.py
@@ -40,32 +40,17 @@
             out[base + count + quarter : base + 2 * count, :] = high[:, lanes]
 
 
-def forward_kernel(n_x, cols, own, low, high, weights, partial, x_rows, g_rows, held, arrived):
-    y = pl.program_id(0)
+def forward_kernel(n_x, cols, own, low, high, weights, partial, x_rows, g_rows):
     ff = weights.shape[3]
 
-    def copies(step):
-        return [
-            pltpu.make_async_copy(
-                weights.at[step, k],
-                held.at[step, :, k * ff : (k + 1) * ff],
-                arrived.at[step, k],
-            )
-            for k in range(3)
-        ]
-
-    @pl.when(y == 0)
+    @pl.when(pl.program_id(0) == 0)
     def _():
-        for step in range(held.shape[0]):
-            for copy in copies(step):
-                copy.start()
         gather_rows(n_x, cols, own, low, high, (x_rows, g_rows))
 
-    for copy in copies(y):
-        copy.wait()
-    first = jnp.dot(x_rows[...], held[y, :, : 2 * ff], preferred_element_type=F32)
+    pair = jnp.concatenate([weights[0, 0], weights[0, 1]], axis=1)
+    first = jnp.dot(x_rows[...], pair, preferred_element_type=F32)
     partial[:, : 2 * ff] = first.astype(BF16)
-    second = jnp.dot(g_rows[...], held[y, :, 2 * ff :], preferred_element_type=F32)
+    second = jnp.dot(g_rows[...], weights[0, 2], preferred_element_type=F32)
     partial[:, 2 * ff :] = second.astype(BF16)
 
 
@@ -79,16 +64,11 @@
             whole(own.shape),
             whole(low.shape),
             whole(high.shape),
-            pl.BlockSpec(memory_space=pltpu.HBM),
+            pl.BlockSpec((1, three, cols, ff), lambda y: (y, 0, 0, 0)),
         ],
         out_specs=pl.BlockSpec((rows, three * ff), lambda y: (0, y)),
         out_shape=pltpu.HBM((rows, n_y * three * ff), BF16),
-        scratch_shapes=[
-            pltpu.VMEM((rows, cols), BF16),
-            pltpu.VMEM((rows, cols), BF16),
-            pltpu.VMEM((n_y, cols, three * ff), BF16),
-            pltpu.SemaphoreType.DMA((n_y, three)),
-        ],
+        scratch_shapes=[pltpu.VMEM((rows, cols), BF16), pltpu.VMEM((rows, cols), BF16)],
         compiler_params=params(),
         cost_estimate=pl.CostEstimate(
             flops=2 * rows * cols * n_y * three * ff, bytes_accessed=7_000_000, transcendentals=0
@@ -295,26 +275,30 @@
     grads, score = hidden_part(upper_half[None], partial, own, low, high, n_y)
     grads = exchange(grads, "dp").reshape(n_x * all_rows, -1)
 
-    total = weight_grad(own, low, high, grads, n_x, n_y, cols)
-    total, grads = lax.optimization_barrier((total, grads))
-    total = lax.psum_scatter(total, "expert", scatter_dimension=0, axis_index_groups=along_y)
-
     mine, send_up, send_down = input_grad(grads, weights, score, n_x)
+    send_up, send_down, grads = lax.optimization_barrier((send_up, send_down, grads))
     from_below = lax.ppermute(send_up, "expert", up_z)
     from_above = lax.ppermute(send_down, "expert", down_z)
+
+    total = weight_grad(own, low, high, grads, n_x, n_y, cols)
+    from_below, from_above, _ = lax.optimization_barrier((from_below, from_above, total))
+    total = lax.psum_scatter(total, "expert", scatter_dimension=0, axis_index_groups=along_y)
+
     back = mine.astype(F32) + jnp.concatenate([from_below, from_above], axis=0).astype(F32)
     back = exchange(back.astype(BF16).reshape(half, tok, -1), "expert", same_parity)
     back = jnp.sum(back.astype(F32), axis=0)
-    back, total = lax.optimization_barrier((back, total))
-    grads = [total[k : k + 1].astype(F32) for k in range(3)]
     score = back[:, width : width + experts]
     grad_combine = jnp.sum(jnp.where(chosen, score[:, None, :], 0.0), axis=2)[None]
+    back, grad_combine, total = lax.optimization_barrier((back, grad_combine, total))
+    grads = [total[k : k + 1].astype(F32) for k in range(3)]
     passed = jnp.stack([back[:, x * cols : (x + 1) * cols] for x in range(n_x)])
-    passed = exchange(passed.astype(BF16), "dp")
+    sections = lax.axis_size("pipe")
+    passed = jnp.broadcast_to(passed.astype(BF16)[None], (sections,) + passed.shape)
+    passed = exchange(passed.reshape(sections * n_x, tok, cols), ("pipe", "dp"))
+    passed, grads = lax.optimization_barrier((passed, grads))
+    source = (lax.axis_index("pipe") + 1) % sections
+    passed = lax.dynamic_slice_in_dim(passed, source * n_x, n_x, 0)
     passed = jnp.concatenate([passed[x] for x in range(n_x)], axis=1)[None]
-    passed, grads = lax.optimization_barrier((passed, grads))
-    sections = lax.axis_size("pipe")
-    passed = lax.ppermute(passed, "pipe", [(s, (s - 1) % sections) for s in range(sections)])
     return passed, grad_combine, *grads
 
 

time: 196 us -> 193 us (0.985)
  blocking collectives: 92.3 us -> 51.9 us
  starting transfers between devices: 35.8 us -> 55.9 us
  waiting for transfers between devices: 28.7 us -> 47.1 us
    all_to_all x2 -> x1, blocking collectives: 56.7 us -> 16.3 us  [exchange(): lax.all_to_all(blocks, axis, 0, 0, axis_index_groups=groups, tiled=True)]
    all_to_all x3 -> x4, starting transfers between devices: 11.7 us -> 41.4 us  [exchange(): lax.all_to_all(blocks, axis, 0, 0, axis_index_groups=groups, tiled=True)]
    all_to_all x3 -> x4, waiting for transfers between devices: 17.1 us -> 36.3 us  [exchange(): lax.all_to_all(blocks, axis, 0, 0, axis_index_groups=groups, tiled=True)]
    ppermute x1 -> x0, starting transfers between devices: 9.49 us -> none  [body(): lax.ppermute(passed, 'pipe', [(s, (s - 1) % sections) for s in range(sect...]
    ppermute x1, waiting for transfers between devices: 4.87 us -> 0.76 us  [body(): high = lax.ppermute(own[own_rows // 2:], 'expert', down_z)]
    ppermute x1, starting transfers between devices: 7.18 us -> 4.5 us  [body(): from_above = lax.ppermute(send_down, 'expert', down_z)]
    unnamed x17 -> x16, local copies, waits for them, and re-layouts: 4.24 us -> 1.85 us
    reduce_scatter x1, waiting for transfers between devices: 0.02 us -> 2.25 us  [body(): lax.psum_scatter(total, 'expert', scatter_dimension=0, axis_index_groups=...]
  transfers between devices with their start and end apart: 10 -> 10, of which waited for: 8 -> 9; matrix products, arithmetic and copies ran while one was open for 3% -> 3% of each run, Pallas kernels for 1% -> 0%
where the time goes in v4:
time: 193 us; the launch traced here: 192 us
  starting transfers between devices  55.9 us (29%)
  blocking collectives  51.9 us (27%)
  waiting for transfers between devices  47.1 us (24%)
  between operations  14.2 us (7%)
  Pallas kernels  12.1 us (6%)
  other arithmetic  8.3 us (4%)
  local copies, waits for them, and re-layouts  2.61 us (1%)
    all_to_all x4, starting transfers between devices, exchange(): lax.all_to_all(blocks, axis, 0, 0, axis_index_groups=groups, tiled=True)  41.4 us
    all_to_all x4, waiting for transfers between devices, exchange(): lax.all_to_all(blocks, axis, 0, 0, axis_index_groups=groups, tiled=True)  36.3 us
    all_gather x1, blocking collectives, body(): lax.all_gather(line, 'expert', axis_index_groups=same_parity, tiled=True)  35.6 us
    all_to_all x1, blocking collectives, exchange(): lax.all_to_all(blocks, axis, 0, 0, axis_index_groups=groups, tiled=True)  16.3 us
    ppermute x1, waiting for transfers between devices, body(): low = lax.ppermute(own[:own_rows // 2], 'expert', up_z)  4.73 us
    ppermute x1, starting transfers between devices, body(): from_above = lax.ppermute(send_down, 'expert', down_z)  4.5 us
    ppermute x1, starting transfers between devices, body(): high = lax.ppermute(own[own_rows // 2:], 'expert', down_z)  4.23 us
    pallas_call x1, Pallas kernels, weight_grad(): pl.pallas_call(functools.partial(weight_kernel, n_x, cols), grid=(n_y,),...  4.08 us
  transfers between devices with their start and end apart: 10, of which 9 were waited for; matrix products, arithmetic and copies ran while one was open for 3% of the time, Pallas kernels for 0%

profile of v4, /device:TPU:1, one launch (start us, length us, event | category | flops | bytes accessed | tf_op | source)
XLA Modules:
  0.0 192.1 jit_solution(17172045204210121387)
XLA Ops:
  8.7 4.8 %all-to-all-start = ((bf16[4,16,896]{2,1,0:T(8,128)(2,1)}), bf16[4,16,896]{2,1,0:T(8,128)(2,1)S(1)}, u32[]{:S(2)}, u32[]{:S(2)}) async-start(bf16[4,16,896]{2,1,0:T(8,128)(2,1)} %maximum_bitcast_fusion), calls=%async_computation | async-start | bytes 229376 | tf_op jit(solution)/shard_map/all_to_all | solution.py:18
  13.5 2.1 %pad_maximum_fusion = bf16[3,896,128]{2,1,0:T(8,128)(2,1)} fusion(bf16[1,896,128]{2,1,0:T(8,128)(2,1)} %param.13, bf16[1,896,128]{2,1,0:T(8,128)(2,1)} %param.12, bf16[1,896,128]{2,1,0:T(8,128)(2,1)} %param.11), kind=kLoop, calls=%fused_computation.2 | loop fusion | flops 688128 | bytes 1376256 | tf_op jit(solution)/shard_map/stack | solution.py:260
  15.8 2.5 %all-to-all-done = bf16[4,16,896]{2,1,0:T(8,128)(2,1)S(1)} async-done(((bf16[4,16,896]{2,1,0:T(8,128)(2,1)}), bf16[4,16,896]{2,1,0:T(8,128)(2,1)S(1)}, u32[]{:S(2)}, u32[]{:S(2)}) %all-to-all-start) | async-done | bytes 114720 | tf_op jit(solution)/shard_map/all_to_all | solution.py:18
  18.4 35.6 %all_gather.9.own = bf16[64,7296]{1,0:T(8,128)(2,1)S(1)} all-gather(bf16[8,7296]{1,0:T(8,128)(2,1)S(1)} %constant_dynamic-update-slice_fusion), channel_id=1, replica_groups={{0,8,16,24,32,40,48,56},{4,12,20,28,36,44,52,60},{64,72,80,88,96,104,11..., dimensions={0}, use_global_device_ids=true | all-gather | bytes 1050624 | tf_op jit(solution)/shard_map/all_gather | solution.py:270
  54.0 2.3 %collective-permute-start = (bf16[32,7296]{1,0:T(8,128)(2,1)S(1)}, bf16[32,7296]{1,0:T(8,128)(2,1)S(1)}, u32[]{:S(2)}, u32[]{:S(2)}) collective-permute-start(bf16[32,7296]{1,0:T(8,128)(2,1)S(1)} %get-tuple-element.48), channel_id=1, source_target_pairs={{0,4},{4,8},{8,12},{12,16},{16,20},{20,24},{24,28},{28,32},{32,36}... | collective-permute-start | bytes 1400840 | tf_op jit(solution)/shard_map/ppermute | solution.py:271
  56.3 4.2 %collective-permute-start.1 = (bf16[32,7296]{1,0:T(8,128)(2,1)S(1)}, bf16[32,7296]{1,0:T(8,128)(2,1)S(1)}, u32[]{:S(2)}, u32[]{:S(2)}) collective-permute-start(bf16[32,7296]{1,0:T(8,128)(2,1)S(1)} %get-tuple-element.47), channel_id=1, source_target_pairs={{4,0},{8,4},{12,8},{16,12},{20,16},{24,20},{28,24},{32,28},{36,32}... | collective-permute-start | bytes 1400840 | tf_op jit(solution)/shard_map/ppermute | solution.py:272
  60.5 4.7 %collective-permute-done.low = bf16[32,7296]{1,0:T(8,128)(2,1)S(1)} collective-permute-done((bf16[32,7296]{1,0:T(8,128)(2,1)S(1)}, bf16[32,7296]{1,0:T(8,128)(2,1)S(1)}, u32[]{:S(2)}, u32[]{:S(2)}) %collective-permute-start) | collective-permute-done | bytes 466976 | tf_op jit(solution)/shard_map/ppermute | solution.py:271
  66.0 1.8 copy-done
  67.8 3.7 %shard_map.110 = bf16[512,1536]{1,0:T(8,128)(2,1)} custom-call(bf16[64,7296]{1,0:T(8,128)(2,1)S(1)} %all_gather.9.own, bf16[32,7296]{1,0:T(8,128)(2,1)S(1)} %collective-permute-done.low, bf16[32,7296]{1,0:T(8,128)(2,1)S(1)} %collective-permute-done.1.high, bf16[4,3,896,128]{3,2,1,0:T(8,128)(2,1)S(1)} %bitcast.69), custom_call_target="tpu_custom_call" | custom-call | flops 1409286144 | bytes 7000000 | tf_op jit(solution)/shard_map/pallas_call | solution.py:60
  71.5 3.7 %all-to-all-start.1 = ((bf16[4,128,1536]{2,1,0:T(8,128)(2,1)}), bf16[4,128,1536]{2,1,0:T(8,128)(2,1)S(1)}, u32[]{:S(2)}, u32[]{:S(2)}) async-start(bf16[4,128,1536]{2,1,0:T(8,128)(2,1)} %bitcast.71), calls=%async_computation.1 | async-start | bytes 3145728 | tf_op jit(solution)/shard_map/all_to_all | solution.py:18
  75.2 12.5 %all-to-all-done.1.partial = bf16[4,128,1536]{2,1,0:T(8,128)(2,1)S(1)} async-done(((bf16[4,128,1536]{2,1,0:T(8,128)(2,1)}), bf16[4,128,1536]{2,1,0:T(8,128)(2,1)S(1)}, u32[]{:S(2)}, u32[]{:S(2)}) %all-to-all-start.1) | async-done | bytes 1572896 | tf_op jit(solution)/shard_map/all_to_all | solution.py:18
  87.8 2.4 %shard_map.111 = (bf16[4,128,1536]{2,1,0:T(8,128)(2,1)}, bf16[128,128]{1,0:T(8,128)(2,1)S(1)}) custom-call(s32[1]{0:T(128)} %bitcast.half, bf16[4,128,1536]{2,1,0:T(8,128)(2,1)S(1)} %all-to-all-done.1.partial, bf16[64,7296]{1,0:T(8,128)(2,1)S(1)} %all_gather.9.own, bf16[32,7296]{1,0:T(8,128)(2,1)S(1)} %collective-permute-done.low, ...), custom_call_target="tpu_custom_call" | custom-call | flops 3932160 | bytes 3145728 | tf_op jit(solution)/shard_map/pallas_call | solution.py:122
  90.2 16.3 %all_to_all.25 = bf16[4,128,1536]{2,1,0:T(8,128)(2,1)S(1)} all-to-all(bf16[4,128,1536]{2,1,0:T(8,128)(2,1)} %get-tuple-element.30), channel_id=1, replica_groups=mesh['pipe'=2,'expert'=64,'dp'=4] {'dp'}, dimensions={0} | all-to-all | bytes 3145728 | tf_op jit(solution)/shard_map/all_to_all | solution.py:18
  106.5 1.9 %shard_map.112 = (bf16[64,3712]{1,0:T(8,128)(2,1)S(1)}, bf16[32,3712]{1,0:T(8,128)(2,1)S(1)}, bf16[32,3712]{1,0:T(8,128)(2,1)S(1)}) custom-call(bf16[512,1536]{1,0:T(8,128)(2,1)S(1)} %bitcast.67, bf16[4,3,896,128]{3,2,1,0:T(8,128)(2,1)S(1)} %bitcast.70, bf16[128,128]{1,0:T(8,128)(2,1)S(1)} %get-tuple-element.31.score), custom_call_target="tpu_custom_call" | custom-call | flops 939524096 | bytes 6000000 | tf_op jit(solution)/shard_map/pallas_call | solution.py:182
  108.4 4.1 %shard_map.113 = bf16[4,3,896,128]{3,2,1,0:T(8,128)(2,1)} custom-call(bf16[64,7296]{1,0:T(8,128)(2,1)S(1)} %all_gather.9.own, bf16[32,7296]{1,0:T(8,128)(2,1)S(1)} %collective-permute-done.low, bf16[32,7296]{1,0:T(8,128)(2,1)S(1)} %collective-permute-done.1.high, bf16[512,1536]{1,0:T(8,128)(2,1)S(1)} %bitcast.68), custom_call_target="tpu_custom_call" | custom-call | flops 1409286144 | bytes 7000000 | tf_op jit(solution)/shard_map/pallas_call | solution.py:220
  112.5 3.6 %collective-permute-start.2 = (bf16[32,3712]{1,0:T(8,128)(2,1)S(1)}, bf16[32,3712]{1,0:T(8,128)(2,1)S(1)}, u32[]{:S(2)}, u32[]{:S(2)}) collective-permute-start(bf16[32,3712]{1,0:T(8,128)(2,1)S(1)} %get-tuple-element.35), channel_id=1, source_target_pairs={{0,4},{4,8},{8,12},{12,16},{16,20},{20,24},{24,28},{28,32},{32,36}... | collective-permute-start | bytes 712712 | tf_op jit(solution)/shard_map/ppermute | solution.py:280
  116.1 4.5 %collective-permute-start.3 = (bf16[32,3712]{1,0:T(8,128)(2,1)S(1)}, bf16[32,3712]{1,0:T(8,128)(2,1)S(1)}, u32[]{:S(2)}, u32[]{:S(2)}) collective-permute-start(bf16[32,3712]{1,0:T(8,128)(2,1)S(1)} %get-tuple-element.36), channel_id=1, source_target_pairs={{4,0},{8,4},{12,8},{16,12},{20,16},{24,20},{28,24},{32,28},{36,32}... | collective-permute-start | bytes 712712 | tf_op jit(solution)/shard_map/ppermute | solution.py:281
  120.6 1.6 collective-permute-done.2
  124.6 19.7 %all-to-all-start.3 = ((bf16[8,8,3712]{2,1,0:T(8,128)(2,1)}), bf16[8,8,3712]{2,1,0:T(8,128)(2,1)S(1)}, u32[]{:S(2)}, u32[]{:S(2)}) async-start(bf16[8,8,3712]{2,1,0:T(8,128)(2,1)} %fusion), calls=%async_computation.3 | async-start | bytes 950272 | tf_op jit(solution)/shard_map/all_to_all | solution.py:18
  144.3 18.4 %all-to-all-done.3 = bf16[8,8,3712]{2,1,0:T(8,128)(2,1)S(1)} async-done(((bf16[8,8,3712]{2,1,0:T(8,128)(2,1)}), bf16[8,8,3712]{2,1,0:T(8,128)(2,1)S(1)}, u32[]{:S(2)}, u32[]{:S(2)}) %all-to-all-start.3) | async-done | bytes 475168 | tf_op jit(solution)/shard_map/all_to_all | solution.py:18
  163.5 2.2 %reduce-scatter.2.cloned.1.call-done = bf16[1,3,896,128]{3,2,1,0:T(8,128)(2,1)} async-done(((bf16[4,3,896,128]{3,2,1,0:T(8,128)(2,1)}), bf16[1,3,896,128]{3,2,1,0:T(8,128)(2,1)}) %reduce-scatter.2.cloned.1.call-update) | async-done | bytes 688144 | tf_op jit(solution)/shard_map/reduce_scatter | solution.py:285
  166.4 13.1 %all-to-all-start.4 = ((bf16[8,8,896]{2,1,0:T(8,128)(2,1)}), bf16[8,8,896]{2,1,0:T(8,128)(2,1)S(1)}, u32[]{:S(2)}, u32[]{:S(2)}) async-start(bf16[8,8,896]{2,1,0:T(8,128)(2,1)} %bitcast.24), calls=%async_computation.5 | async-start | bytes 229376 | tf_op jit(solution)/shard_map/all_to_all | solution.py:18
  179.6 2.3 %slice_convert_fusion = (f32[1,896,128]{2,1,0:T(8,128)}, f32[1,896,128]{2,1,0:T(8,128)}, f32[1,896,128]{2,1,0:T(8,128)}) fusion(bf16[3,896,128]{2,1,0:T(8,128)(2,1)} %bitcast.72), kind=kLoop, calls=%fused_computation.4 | loop fusion | flops 344064 | bytes 2064384 | tf_op jit(solution)/shard_map/convert_element_type | solution.py:293
  181.8 2.8 %all-to-all-done.4 = bf16[8,8,896]{2,1,0:T(8,128)(2,1)S(1)} async-done(((bf16[8,8,896]{2,1,0:T(8,128)(2,1)}), bf16[8,8,896]{2,1,0:T(8,128)(2,1)S(1)}, u32[]{:S(2)}, u32[]{:S(2)}) %all-to-all-start.4) | async-done | bytes 114720 | tf_op jit(solution)/shard_map/all_to_all | solution.py:18
  (37 shorter events, 7.1 us)
Async XLA Ops:
  7.2 8.5 %copy-start.3 = (bf16[1,8,4]{1,2,0:T(4,128)(2,1)S(1)}, bf16[1,8,4]{1,2,0:T(4,128)(2,1)}, u32[]{:S(2)}) copy-start(bf16[1,8,4]{1,2,0:T(4,128)(2,1)} %param.10) | copy-start | bytes 196
  7.2 8.5 %copy-start.2 = (s32[1,8,4]{1,2,0:T(4,128)S(1)}, s32[1,8,4]{1,2,0:T(4,128)}, u32[]{:S(2)}) copy-start(s32[1,8,4]{1,2,0:T(4,128)} %param.9) | copy-start | bytes 388
  8.7 9.6 %all-to-all-start = ((bf16[4,16,896]{2,1,0:T(8,128)(2,1)}), bf16[4,16,896]{2,1,0:T(8,128)(2,1)S(1)}, u32[]{:S(2)}, u32[]{:S(2)}) async-start(bf16[4,16,896]{2,1,0:T(8,128)(2,1)} %maximum_bitcast_fusion), calls=%async_computation | async-start | bytes 229376 | tf_op jit(solution)/shard_map/all_to_all | solution.py:18
  13.5 52.5 %all-gather.3.cloned.1.call-start = ((), (), s32[]{:S(2)}) async-start(), calls=%async_computation.7 | async-start | bytes 3440640 | tf_op jit(solution)/shard_map/all_gather | solution.py:261
  54.0 11.2 %collective-permute-start = (bf16[32,7296]{1,0:T(8,128)(2,1)S(1)}, bf16[32,7296]{1,0:T(8,128)(2,1)S(1)}, u32[]{:S(2)}, u32[]{:S(2)}) collective-permute-start(bf16[32,7296]{1,0:T(8,128)(2,1)S(1)} %get-tuple-element.48), channel_id=1, source_target_pairs={{0,4},{4,8},{8,12},{12,16},{16,20},{20,24},{24,28},{28,32},{32,36}... | collective-permute-start | bytes 1400840 | tf_op jit(solution)/shard_map/ppermute | solution.py:271
  56.3 9.7 %collective-permute-start.1 = (bf16[32,7296]{1,0:T(8,128)(2,1)S(1)}, bf16[32,7296]{1,0:T(8,128)(2,1)S(1)}, u32[]{:S(2)}, u32[]{:S(2)}) collective-permute-start(bf16[32,7296]{1,0:T(8,128)(2,1)S(1)} %get-tuple-element.47), channel_id=1, source_target_pairs={{4,0},{8,4},{12,8},{16,12},{20,16},{24,20},{28,24},{32,28},{36,32}... | collective-permute-start | bytes 1400840 | tf_op jit(solution)/shard_map/ppermute | solution.py:272
  66.0 1.8 copy-start
  71.5 16.3 %all-to-all-start.1 = ((bf16[4,128,1536]{2,1,0:T(8,128)(2,1)}), bf16[4,128,1536]{2,1,0:T(8,128)(2,1)S(1)}, u32[]{:S(2)}, u32[]{:S(2)}) async-start(bf16[4,128,1536]{2,1,0:T(8,128)(2,1)} %bitcast.71), calls=%async_computation.1 | async-start | bytes 3145728 | tf_op jit(solution)/shard_map/all_to_all | solution.py:18
  75.2 90.5 %reduce-scatter.2.cloned.1.call-start = ((), (), s32[]{:S(2)}) async-start(), calls=%async_computation.6 | async-start | bytes 3440640 | tf_op jit(solution)/shard_map/reduce_scatter | solution.py:285
  90.2 16.3 %copy-start.1 = (bf16[12,896,128]{2,1,0:T(8,128)(2,1)S(1)}, bf16[12,896,128]{2,1,0:T(8,128)(2,1)}, u32[]{:S(2)}) copy-start(bf16[12,896,128]{2,1,0:T(8,128)(2,1)} %all-gather.3.cloned.1.call-done) | copy-start | bytes 8257540
  112.5 9.6 %collective-permute-start.2 = (bf16[32,3712]{1,0:T(8,128)(2,1)S(1)}, bf16[32,3712]{1,0:T(8,128)(2,1)S(1)}, u32[]{:S(2)}, u32[]{:S(2)}) collective-permute-start(bf16[32,3712]{1,0:T(8,128)(2,1)S(1)} %get-tuple-element.35), channel_id=1, source_target_pairs={{0,4},{4,8},{8,12},{12,16},{16,20},{20,24},{24,28},{28,32},{32,36}... | collective-permute-start | bytes 712712 | tf_op jit(solution)/shard_map/ppermute | solution.py:280
  116.1 7.5 %collective-permute-start.3 = (bf16[32,3712]{1,0:T(8,128)(2,1)S(1)}, bf16[32,3712]{1,0:T(8,128)(2,1)S(1)}, u32[]{:S(2)}, u32[]{:S(2)}) collective-permute-start(bf16[32,3712]{1,0:T(8,128)(2,1)S(1)} %get-tuple-element.36), channel_id=1, source_target_pairs={{4,0},{8,4},{12,8},{16,12},{20,16},{24,20},{28,24},{32,28},{36,32}... | collective-permute-start | bytes 712712 | tf_op jit(solution)/shard_map/ppermute | solution.py:281
  124.6 38.1 %all-to-all-start.3 = ((bf16[8,8,3712]{2,1,0:T(8,128)(2,1)}), bf16[8,8,3712]{2,1,0:T(8,128)(2,1)S(1)}, u32[]{:S(2)}, u32[]{:S(2)}) async-start(bf16[8,8,3712]{2,1,0:T(8,128)(2,1)} %fusion), calls=%async_computation.3 | async-start | bytes 950272 | tf_op jit(solution)/shard_map/all_to_all | solution.py:18
  166.4 18.2 %all-to-all-start.4 = ((bf16[8,8,896]{2,1,0:T(8,128)(2,1)}), bf16[8,8,896]{2,1,0:T(8,128)(2,1)S(1)}, u32[]{:S(2)}, u32[]{:S(2)}) async-start(bf16[8,8,896]{2,1,0:T(8,128)(2,1)} %bitcast.24), calls=%async_computation.5 | async-start | bytes 229376 | tf_op jit(solution)/shard_map/all_to_all | solution.py:18
Sparse Core Ops, SparseCore 0:
  16.5 49.2 all-gather.2
  112.7 53.0 reduce-scatter.1

commit v5 on v4

--- a/solution.py
+++ b/solution.py
@@ -125,7 +125,7 @@
         in_specs=[pl.BlockSpec(memory_space=pltpu.SMEM), block] + tails,
         out_specs=[block, whole((rows, LANES))],
         out_shape=[
-            pltpu.HBM(partial.shape, BF16),
+            jax.ShapeDtypeStruct(partial.shape, BF16),
             jax.ShapeDtypeStruct((rows, LANES), BF16),
         ],
         compiler_params=params(),

time: 193 us -> 191 us (0.990)
  no operation moved by 1% of the time
where the time goes in v5:
time: 191 us; the launch traced here: 190 us
  starting transfers between devices  54.8 us (29%)
  blocking collectives  52 us (27%)
  waiting for transfers between devices  47.1 us (25%)
  between operations  14.2 us (7%)
  Pallas kernels  11.1 us (6%)
  other arithmetic  8.3 us (4%)
  local copies, waits for them, and re-layouts  2.61 us (1%)
    all_to_all x4, starting transfers between devices, exchange(): lax.all_to_all(blocks, axis, 0, 0, axis_index_groups=groups, tiled=True)  41.4 us
    all_to_all x4, waiting for transfers between devices, exchange(): lax.all_to_all(blocks, axis, 0, 0, axis_index_groups=groups, tiled=True)  36.3 us
    all_gather x1, blocking collectives, body(): lax.all_gather(line, 'expert', axis_index_groups=same_parity, tiled=True)  35.6 us
    all_to_all x1, blocking collectives, exchange(): lax.all_to_all(blocks, axis, 0, 0, axis_index_groups=groups, tiled=True)  16.4 us
    ppermute x1, waiting for transfers between devices, body(): low = lax.ppermute(own[:own_rows // 2], 'expert', up_z)  4.73 us
    ppermute x1, starting transfers between devices, body(): from_above = lax.ppermute(send_down, 'expert', down_z)  4.51 us
    ppermute x1, starting transfers between devices, body(): high = lax.ppermute(own[own_rows // 2:], 'expert', down_z)  4.23 us
    pallas_call x1, Pallas kernels, weight_grad(): pl.pallas_call(functools.partial(weight_kernel, n_x, cols), grid=(n_y,),...  4.09 us
  transfers between devices with their start and end apart: 10, of which 9 were waited for; matrix products, arithmetic and copies ran while one was open for 3% of the time, Pallas kernels for 0%

profile of v5, /device:TPU:1, one launch (start us, length us, event | category | flops | bytes accessed | tf_op | source)
XLA Modules:
  0.0 190.0 jit_solution(1732720461008342112)
XLA Ops:
  7.2 1.5 maximum_bitcast_fusion
  8.7 4.8 %all-to-all-start = ((bf16[4,16,896]{2,1,0:T(8,128)(2,1)}), bf16[4,16,896]{2,1,0:T(8,128)(2,1)S(1)}, u32[]{:S(2)}, u32[]{:S(2)}) async-start(bf16[4,16,896]{2,1,0:T(8,128)(2,1)} %maximum_bitcast_fusion), calls=%async_computation | async-start | bytes 229376 | tf_op jit(solution)/shard_map/all_to_all | solution.py:18
  13.5 2.1 %pad_maximum_fusion = bf16[3,896,128]{2,1,0:T(8,128)(2,1)} fusion(bf16[1,896,128]{2,1,0:T(8,128)(2,1)} %param.13, bf16[1,896,128]{2,1,0:T(8,128)(2,1)} %param.12, bf16[1,896,128]{2,1,0:T(8,128)(2,1)} %param.11), kind=kLoop, calls=%fused_computation.2 | loop fusion | flops 688128 | bytes 1376256 | tf_op jit(solution)/shard_map/stack | solution.py:260
  15.8 2.5 %all-to-all-done = bf16[4,16,896]{2,1,0:T(8,128)(2,1)S(1)} async-done(((bf16[4,16,896]{2,1,0:T(8,128)(2,1)}), bf16[4,16,896]{2,1,0:T(8,128)(2,1)S(1)}, u32[]{:S(2)}, u32[]{:S(2)}) %all-to-all-start) | async-done | bytes 114720 | tf_op jit(solution)/shard_map/all_to_all | solution.py:18
  18.4 35.6 %all_gather.9.own = bf16[64,7296]{1,0:T(8,128)(2,1)S(1)} all-gather(bf16[8,7296]{1,0:T(8,128)(2,1)S(1)} %constant_dynamic-update-slice_fusion), channel_id=1, replica_groups={{0,8,16,24,32,40,48,56},{4,12,20,28,36,44,52,60},{64,72,80,88,96,104,11..., dimensions={0}, use_global_device_ids=true | all-gather | bytes 1050624 | tf_op jit(solution)/shard_map/all_gather | solution.py:270
  54.0 2.3 %collective-permute-start = (bf16[32,7296]{1,0:T(8,128)(2,1)S(1)}, bf16[32,7296]{1,0:T(8,128)(2,1)S(1)}, u32[]{:S(2)}, u32[]{:S(2)}) collective-permute-start(bf16[32,7296]{1,0:T(8,128)(2,1)S(1)} %get-tuple-element.48), channel_id=1, source_target_pairs={{0,4},{4,8},{8,12},{12,16},{16,20},{20,24},{24,28},{28,32},{32,36}... | collective-permute-start | bytes 1400840 | tf_op jit(solution)/shard_map/ppermute | solution.py:271
  56.3 4.2 %collective-permute-start.1 = (bf16[32,7296]{1,0:T(8,128)(2,1)S(1)}, bf16[32,7296]{1,0:T(8,128)(2,1)S(1)}, u32[]{:S(2)}, u32[]{:S(2)}) collective-permute-start(bf16[32,7296]{1,0:T(8,128)(2,1)S(1)} %get-tuple-element.47), channel_id=1, source_target_pairs={{4,0},{8,4},{12,8},{16,12},{20,16},{24,20},{28,24},{32,28},{36,32}... | collective-permute-start | bytes 1400840 | tf_op jit(solution)/shard_map/ppermute | solution.py:272
  60.5 4.7 %collective-permute-done.low = bf16[32,7296]{1,0:T(8,128)(2,1)S(1)} collective-permute-done((bf16[32,7296]{1,0:T(8,128)(2,1)S(1)}, bf16[32,7296]{1,0:T(8,128)(2,1)S(1)}, u32[]{:S(2)}, u32[]{:S(2)}) %collective-permute-start) | collective-permute-done | bytes 466976 | tf_op jit(solution)/shard_map/ppermute | solution.py:271
  66.0 1.8 copy-done
  67.8 3.7 %shard_map.110 = bf16[512,1536]{1,0:T(8,128)(2,1)} custom-call(bf16[64,7296]{1,0:T(8,128)(2,1)S(1)} %all_gather.9.own, bf16[32,7296]{1,0:T(8,128)(2,1)S(1)} %collective-permute-done.low, bf16[32,7296]{1,0:T(8,128)(2,1)S(1)} %collective-permute-done.1.high, bf16[4,3,896,128]{3,2,1,0:T(8,128)(2,1)S(1)} %bitcast.69), custom_call_target="tpu_custom_call" | custom-call | flops 1409286144 | bytes 7000000 | tf_op jit(solution)/shard_map/pallas_call | solution.py:60
  71.5 3.7 %all-to-all-start.1 = ((bf16[4,128,1536]{2,1,0:T(8,128)(2,1)}), bf16[4,128,1536]{2,1,0:T(8,128)(2,1)S(1)}, u32[]{:S(2)}, u32[]{:S(2)}) async-start(bf16[4,128,1536]{2,1,0:T(8,128)(2,1)} %bitcast.71), calls=%async_computation.1 | async-start | bytes 3145728 | tf_op jit(solution)/shard_map/all_to_all | solution.py:18
  75.2 12.5 %all-to-all-done.1.partial = bf16[4,128,1536]{2,1,0:T(8,128)(2,1)S(1)} async-done(((bf16[4,128,1536]{2,1,0:T(8,128)(2,1)}), bf16[4,128,1536]{2,1,0:T(8,128)(2,1)S(1)}, u32[]{:S(2)}, u32[]{:S(2)}) %all-to-all-start.1) | async-done | bytes 1572896 | tf_op jit(solution)/shard_map/all_to_all | solution.py:18
  89.1 16.4 %all_to_all.25 = bf16[4,128,1536]{2,1,0:T(8,128)(2,1)S(1)} all-to-all(bf16[4,128,1536]{2,1,0:T(8,128)(2,1)S(1)} %get-tuple-element.30), channel_id=1, replica_groups=mesh['pipe'=2,'expert'=64,'dp'=4] {'dp'}, dimensions={0} | all-to-all | bytes 3145728 | tf_op jit(solution)/shard_map/all_to_all | solution.py:18
  105.6 1.9 %shard_map.112 = (bf16[64,3712]{1,0:T(8,128)(2,1)S(1)}, bf16[32,3712]{1,0:T(8,128)(2,1)S(1)}, bf16[32,3712]{1,0:T(8,128)(2,1)S(1)}) custom-call(bf16[512,1536]{1,0:T(8,128)(2,1)S(1)} %bitcast.67, bf16[4,3,896,128]{3,2,1,0:T(8,128)(2,1)S(1)} %bitcast.70, bf16[128,128]{1,0:T(8,128)(2,1)S(1)} %get-tuple-element.31.score), custom_call_target="tpu_custom_call" | custom-call | flops 939524096 | bytes 6000000 | tf_op jit(solution)/shard_map/pallas_call | solution.py:182
  107.5 4.1 %shard_map.113 = bf16[4,3,896,128]{3,2,1,0:T(8,128)(2,1)} custom-call(bf16[64,7296]{1,0:T(8,128)(2,1)S(1)} %all_gather.9.own, bf16[32,7296]{1,0:T(8,128)(2,1)S(1)} %collective-permute-done.low, bf16[32,7296]{1,0:T(8,128)(2,1)S(1)} %collective-permute-done.1.high, bf16[512,1536]{1,0:T(8,128)(2,1)S(1)} %bitcast.68), custom_call_target="tpu_custom_call" | custom-call | flops 1409286144 | bytes 7000000 | tf_op jit(solution)/shard_map/pallas_call | solution.py:220
  111.6 2.4 %collective-permute-start.2 = (bf16[32,3712]{1,0:T(8,128)(2,1)S(1)}, bf16[32,3712]{1,0:T(8,128)(2,1)S(1)}, u32[]{:S(2)}, u32[]{:S(2)}) collective-permute-start(bf16[32,3712]{1,0:T(8,128)(2,1)S(1)} %get-tuple-element.35), channel_id=1, source_target_pairs={{0,4},{4,8},{8,12},{12,16},{16,20},{20,24},{24,28},{28,32},{32,36}... | collective-permute-start | bytes 712712 | tf_op jit(solution)/shard_map/ppermute | solution.py:280
  114.0 4.5 %collective-permute-start.3 = (bf16[32,3712]{1,0:T(8,128)(2,1)S(1)}, bf16[32,3712]{1,0:T(8,128)(2,1)S(1)}, u32[]{:S(2)}, u32[]{:S(2)}) collective-permute-start(bf16[32,3712]{1,0:T(8,128)(2,1)S(1)} %get-tuple-element.36), channel_id=1, source_target_pairs={{4,0},{8,4},{12,8},{16,12},{20,16},{24,20},{28,24},{32,28},{36,32}... | collective-permute-start | bytes 712712 | tf_op jit(solution)/shard_map/ppermute | solution.py:281
  118.5 1.6 collective-permute-done.2
  122.5 19.7 %all-to-all-start.3 = ((bf16[8,8,3712]{2,1,0:T(8,128)(2,1)}), bf16[8,8,3712]{2,1,0:T(8,128)(2,1)S(1)}, u32[]{:S(2)}, u32[]{:S(2)}) async-start(bf16[8,8,3712]{2,1,0:T(8,128)(2,1)} %fusion), calls=%async_computation.3 | async-start | bytes 950272 | tf_op jit(solution)/shard_map/all_to_all | solution.py:18
  142.1 18.4 %all-to-all-done.3 = bf16[8,8,3712]{2,1,0:T(8,128)(2,1)S(1)} async-done(((bf16[8,8,3712]{2,1,0:T(8,128)(2,1)}), bf16[8,8,3712]{2,1,0:T(8,128)(2,1)S(1)}, u32[]{:S(2)}, u32[]{:S(2)}) %all-to-all-start.3) | async-done | bytes 475168 | tf_op jit(solution)/shard_map/all_to_all | solution.py:18
  161.3 2.2 %reduce-scatter.2.cloned.1.call-done = bf16[1,3,896,128]{3,2,1,0:T(8,128)(2,1)} async-done(((bf16[4,3,896,128]{3,2,1,0:T(8,128)(2,1)}), bf16[1,3,896,128]{3,2,1,0:T(8,128)(2,1)}) %reduce-scatter.2.cloned.1.call-update) | async-done | bytes 688144 | tf_op jit(solution)/shard_map/reduce_scatter | solution.py:285
  164.3 13.1 %all-to-all-start.4 = ((bf16[8,8,896]{2,1,0:T(8,128)(2,1)}), bf16[8,8,896]{2,1,0:T(8,128)(2,1)S(1)}, u32[]{:S(2)}, u32[]{:S(2)}) async-start(bf16[8,8,896]{2,1,0:T(8,128)(2,1)} %bitcast.24), calls=%async_computation.5 | async-start | bytes 229376 | tf_op jit(solution)/shard_map/all_to_all | solution.py:18
  177.4 2.3 %slice_convert_fusion = (f32[1,896,128]{2,1,0:T(8,128)}, f32[1,896,128]{2,1,0:T(8,128)}, f32[1,896,128]{2,1,0:T(8,128)}) fusion(bf16[3,896,128]{2,1,0:T(8,128)(2,1)} %bitcast.72), kind=kLoop, calls=%fused_computation.4 | loop fusion | flops 344064 | bytes 2064384 | tf_op jit(solution)/shard_map/convert_element_type | solution.py:293
  179.7 2.8 %all-to-all-done.4 = bf16[8,8,896]{2,1,0:T(8,128)(2,1)S(1)} async-done(((bf16[8,8,896]{2,1,0:T(8,128)(2,1)}), bf16[8,8,896]{2,1,0:T(8,128)(2,1)S(1)}, u32[]{:S(2)}, u32[]{:S(2)}) %all-to-all-start.4) | async-done | bytes 114720 | tf_op jit(solution)/shard_map/all_to_all | solution.py:18
  (37 shorter events, 6.9 us)
Async XLA Ops:
  7.2 8.5 %copy-start.3 = (bf16[1,8,4]{1,2,0:T(4,128)(2,1)S(1)}, bf16[1,8,4]{1,2,0:T(4,128)(2,1)}, u32[]{:S(2)}) copy-start(bf16[1,8,4]{1,2,0:T(4,128)(2,1)} %param.10) | copy-start | bytes 196
  7.2 8.5 %copy-start.2 = (s32[1,8,4]{1,2,0:T(4,128)S(1)}, s32[1,8,4]{1,2,0:T(4,128)}, u32[]{:S(2)}) copy-start(s32[1,8,4]{1,2,0:T(4,128)} %param.9) | copy-start | bytes 388
  8.7 9.6 %all-to-all-start = ((bf16[4,16,896]{2,1,0:T(8,128)(2,1)}), bf16[4,16,896]{2,1,0:T(8,128)(2,1)S(1)}, u32[]{:S(2)}, u32[]{:S(2)}) async-start(bf16[4,16,896]{2,1,0:T(8,128)(2,1)} %maximum_bitcast_fusion), calls=%async_computation | async-start | bytes 229376 | tf_op jit(solution)/shard_map/all_to_all | solution.py:18
  13.5 52.5 %all-gather.3.cloned.1.call-start = ((), (), s32[]{:S(2)}) async-start(), calls=%async_computation.7 | async-start | bytes 3440640 | tf_op jit(solution)/shard_map/all_gather | solution.py:261
  54.0 11.2 %collective-permute-start = (bf16[32,7296]{1,0:T(8,128)(2,1)S(1)}, bf16[32,7296]{1,0:T(8,128)(2,1)S(1)}, u32[]{:S(2)}, u32[]{:S(2)}) collective-permute-start(bf16[32,7296]{1,0:T(8,128)(2,1)S(1)} %get-tuple-element.48), channel_id=1, source_target_pairs={{0,4},{4,8},{8,12},{12,16},{16,20},{20,24},{24,28},{28,32},{32,36}... | collective-permute-start | bytes 1400840 | tf_op jit(solution)/shard_map/ppermute | solution.py:271
  56.3 9.7 %collective-permute-start.1 = (bf16[32,7296]{1,0:T(8,128)(2,1)S(1)}, bf16[32,7296]{1,0:T(8,128)(2,1)S(1)}, u32[]{:S(2)}, u32[]{:S(2)}) collective-permute-start(bf16[32,7296]{1,0:T(8,128)(2,1)S(1)} %get-tuple-element.47), channel_id=1, source_target_pairs={{4,0},{8,4},{12,8},{16,12},{20,16},{24,20},{28,24},{32,28},{36,32}... | collective-permute-start | bytes 1400840 | tf_op jit(solution)/shard_map/ppermute | solution.py:272
  66.0 1.8 copy-start
  71.5 16.3 %all-to-all-start.1 = ((bf16[4,128,1536]{2,1,0:T(8,128)(2,1)}), bf16[4,128,1536]{2,1,0:T(8,128)(2,1)S(1)}, u32[]{:S(2)}, u32[]{:S(2)}) async-start(bf16[4,128,1536]{2,1,0:T(8,128)(2,1)} %bitcast.71), calls=%async_computation.1 | async-start | bytes 3145728 | tf_op jit(solution)/shard_map/all_to_all | solution.py:18
  75.2 88.4 %reduce-scatter.2.cloned.1.call-start = ((), (), s32[]{:S(2)}) async-start(), calls=%async_computation.6 | async-start | bytes 3440640 | tf_op jit(solution)/shard_map/reduce_scatter | solution.py:285
  89.1 16.4 %copy-start.1 = (bf16[12,896,128]{2,1,0:T(8,128)(2,1)S(1)}, bf16[12,896,128]{2,1,0:T(8,128)(2,1)}, u32[]{:S(2)}) copy-start(bf16[12,896,128]{2,1,0:T(8,128)(2,1)} %all-gather.3.cloned.1.call-done) | copy-start | bytes 8257540
  111.6 8.5 %collective-permute-start.2 = (bf16[32,3712]{1,0:T(8,128)(2,1)S(1)}, bf16[32,3712]{1,0:T(8,128)(2,1)S(1)}, u32[]{:S(2)}, u32[]{:S(2)}) collective-permute-start(bf16[32,3712]{1,0:T(8,128)(2,1)S(1)} %get-tuple-element.35), channel_id=1, source_target_pairs={{0,4},{4,8},{8,12},{12,16},{16,20},{20,24},{24,28},{28,32},{32,36}... | collective-permute-start | bytes 712712 | tf_op jit(solution)/shard_map/ppermute | solution.py:280
  114.0 7.5 %collective-permute-start.3 = (bf16[32,3712]{1,0:T(8,128)(2,1)S(1)}, bf16[32,3712]{1,0:T(8,128)(2,1)S(1)}, u32[]{:S(2)}, u32[]{:S(2)}) collective-permute-start(bf16[32,3712]{1,0:T(8,128)(2,1)S(1)} %get-tuple-element.36), channel_id=1, source_target_pairs={{4,0},{8,4},{12,8},{16,12},{20,16},{24,20},{28,24},{32,28},{36,32}... | collective-permute-start | bytes 712712 | tf_op jit(solution)/shard_map/ppermute | solution.py:281
  122.5 38.1 %all-to-all-start.3 = ((bf16[8,8,3712]{2,1,0:T(8,128)(2,1)}), bf16[8,8,3712]{2,1,0:T(8,128)(2,1)S(1)}, u32[]{:S(2)}, u32[]{:S(2)}) async-start(bf16[8,8,3712]{2,1,0:T(8,128)(2,1)} %fusion), calls=%async_computation.3 | async-start | bytes 950272 | tf_op jit(solution)/shard_map/all_to_all | solution.py:18
  164.3 18.2 %all-to-all-start.4 = ((bf16[8,8,896]{2,1,0:T(8,128)(2,1)}), bf16[8,8,896]{2,1,0:T(8,128)(2,1)S(1)}, u32[]{:S(2)}, u32[]{:S(2)}) async-start(bf16[8,8,896]{2,1,0:T(8,128)(2,1)} %bitcast.24), calls=%async_computation.5 | async-start | bytes 229376 | tf_op jit(solution)/shard_map/all_to_all | solution.py:18
Sparse Core Ops, SparseCore 0:
  16.5 49.2 all-gather.2
  111.7 51.8 reduce-scatter.1

commit v6 on v5

--- a/solution.py
+++ b/solution.py
@@ -24,7 +24,7 @@
 
 def params():
     return pltpu.CompilerParams(
-        dimension_semantics=("arbitrary",), vmem_limit_bytes=20 * 1024 * 1024
+        dimension_semantics=("arbitrary",), vmem_limit_bytes=12 * 1024 * 1024
     )
 
 
@@ -189,7 +189,7 @@
             pltpu.VMEM((n_y, cols, 2 * ff), BF16),
             pltpu.SemaphoreType.DMA((n_y, 2)),
         ],
-        compiler_params=pltpu.CompilerParams(vmem_limit_bytes=20 * 1024 * 1024),
+        compiler_params=pltpu.CompilerParams(vmem_limit_bytes=12 * 1024 * 1024),
         cost_estimate=pl.CostEstimate(
             flops=4 * n_x * rows * cols * n_y * ff, bytes_accessed=6_000_000, transcendentals=0
         ),

time: 191 us -> 191 us (level)
  no operation moved by 1% of the time
where the time goes in v6:
time: 191 us; the launch traced here: 190 us
  starting transfers between devices  54.8 us (29%)
  blocking collectives  52 us (27%)
  waiting for transfers between devices  47.1 us (25%)
  between operations  14.2 us (7%)
  Pallas kernels  11.1 us (6%)
  other arithmetic  8.3 us (4%)
  local copies, waits for them, and re-layouts  2.61 us (1%)
    all_to_all x4, starting transfers between devices, exchange(): lax.all_to_all(blocks, axis, 0, 0, axis_index_groups=groups, tiled=True)  41.4 us
    all_to_all x4, waiting for transfers between devices, exchange(): lax.all_to_all(blocks, axis, 0, 0, axis_index_groups=groups, tiled=True)  36.3 us
    all_gather x1, blocking collectives, body(): lax.all_gather(line, 'expert', axis_index_groups=same_parity, tiled=True)  35.6 us
    all_to_all x1, blocking collectives, exchange(): lax.all_to_all(blocks, axis, 0, 0, axis_index_groups=groups, tiled=True)  16.4 us
    ppermute x1, waiting for transfers between devices, body(): low = lax.ppermute(own[:own_rows // 2], 'expert', up_z)  4.73 us
    ppermute x1, starting transfers between devices, body(): from_above = lax.ppermute(send_down, 'expert', down_z)  4.51 us
    ppermute x1, starting transfers between devices, body(): high = lax.ppermute(own[own_rows // 2:], 'expert', down_z)  4.23 us
    pallas_call x1, Pallas kernels, weight_grad(): pl.pallas_call(functools.partial(weight_kernel, n_x, cols), grid=(n_y,),...  4.09 us
  transfers between devices with their start and end apart: 10, of which 9 were waited for; matrix products, arithmetic and copies ran while one was open for 3% of the time, Pallas kernels for 0%

profile of v6, /device:TPU:1, one launch (start us, length us, event | category | flops | bytes accessed | tf_op | source)
XLA Modules:
  0.0 190.0 jit_solution(2128788346304377515)
XLA Ops:
  7.2 1.5 maximum_bitcast_fusion
  8.7 4.8 %all-to-all-start = ((bf16[4,16,896]{2,1,0:T(8,128)(2,1)}), bf16[4,16,896]{2,1,0:T(8,128)(2,1)S(1)}, u32[]{:S(2)}, u32[]{:S(2)}) async-start(bf16[4,16,896]{2,1,0:T(8,128)(2,1)} %maximum_bitcast_fusion), calls=%async_computation | async-start | bytes 229376 | tf_op jit(solution)/shard_map/all_to_all | solution.py:18
  13.5 2.1 %pad_maximum_fusion = bf16[3,896,128]{2,1,0:T(8,128)(2,1)} fusion(bf16[1,896,128]{2,1,0:T(8,128)(2,1)} %param.13, bf16[1,896,128]{2,1,0:T(8,128)(2,1)} %param.12, bf16[1,896,128]{2,1,0:T(8,128)(2,1)} %param.11), kind=kLoop, calls=%fused_computation.2 | loop fusion | flops 688128 | bytes 1376256 | tf_op jit(solution)/shard_map/stack | solution.py:260
  15.8 2.5 %all-to-all-done = bf16[4,16,896]{2,1,0:T(8,128)(2,1)S(1)} async-done(((bf16[4,16,896]{2,1,0:T(8,128)(2,1)}), bf16[4,16,896]{2,1,0:T(8,128)(2,1)S(1)}, u32[]{:S(2)}, u32[]{:S(2)}) %all-to-all-start) | async-done | bytes 114720 | tf_op jit(solution)/shard_map/all_to_all | solution.py:18
  18.4 35.6 %all_gather.9.own = bf16[64,7296]{1,0:T(8,128)(2,1)S(1)} all-gather(bf16[8,7296]{1,0:T(8,128)(2,1)S(1)} %constant_dynamic-update-slice_fusion), channel_id=1, replica_groups={{0,8,16,24,32,40,48,56},{4,12,20,28,36,44,52,60},{64,72,80,88,96,104,11..., dimensions={0}, use_global_device_ids=true | all-gather | bytes 1050624 | tf_op jit(solution)/shard_map/all_gather | solution.py:270
  54.0 2.3 %collective-permute-start = (bf16[32,7296]{1,0:T(8,128)(2,1)S(1)}, bf16[32,7296]{1,0:T(8,128)(2,1)S(1)}, u32[]{:S(2)}, u32[]{:S(2)}) collective-permute-start(bf16[32,7296]{1,0:T(8,128)(2,1)S(1)} %get-tuple-element.48), channel_id=1, source_target_pairs={{0,4},{4,8},{8,12},{12,16},{16,20},{20,24},{24,28},{28,32},{32,36}... | collective-permute-start | bytes 1400840 | tf_op jit(solution)/shard_map/ppermute | solution.py:271
  56.3 4.2 %collective-permute-start.1 = (bf16[32,7296]{1,0:T(8,128)(2,1)S(1)}, bf16[32,7296]{1,0:T(8,128)(2,1)S(1)}, u32[]{:S(2)}, u32[]{:S(2)}) collective-permute-start(bf16[32,7296]{1,0:T(8,128)(2,1)S(1)} %get-tuple-element.47), channel_id=1, source_target_pairs={{4,0},{8,4},{12,8},{16,12},{20,16},{24,20},{28,24},{32,28},{36,32}... | collective-permute-start | bytes 1400840 | tf_op jit(solution)/shard_map/ppermute | solution.py:272
  60.5 4.7 %collective-permute-done.low = bf16[32,7296]{1,0:T(8,128)(2,1)S(1)} collective-permute-done((bf16[32,7296]{1,0:T(8,128)(2,1)S(1)}, bf16[32,7296]{1,0:T(8,128)(2,1)S(1)}, u32[]{:S(2)}, u32[]{:S(2)}) %collective-permute-start) | collective-permute-done | bytes 466976 | tf_op jit(solution)/shard_map/ppermute | solution.py:271
  66.0 1.8 copy-done
  67.8 3.7 %shard_map.110 = bf16[512,1536]{1,0:T(8,128)(2,1)} custom-call(bf16[64,7296]{1,0:T(8,128)(2,1)S(1)} %all_gather.9.own, bf16[32,7296]{1,0:T(8,128)(2,1)S(1)} %collective-permute-done.low, bf16[32,7296]{1,0:T(8,128)(2,1)S(1)} %collective-permute-done.1.high, bf16[4,3,896,128]{3,2,1,0:T(8,128)(2,1)S(1)} %bitcast.69), custom_call_target="tpu_custom_call" | custom-call | flops 1409286144 | bytes 7000000 | tf_op jit(solution)/shard_map/pallas_call | solution.py:60
  71.5 3.7 %all-to-all-start.1 = ((bf16[4,128,1536]{2,1,0:T(8,128)(2,1)}), bf16[4,128,1536]{2,1,0:T(8,128)(2,1)S(1)}, u32[]{:S(2)}, u32[]{:S(2)}) async-start(bf16[4,128,1536]{2,1,0:T(8,128)(2,1)} %bitcast.71), calls=%async_computation.1 | async-start | bytes 3145728 | tf_op jit(solution)/shard_map/all_to_all | solution.py:18
  75.2 12.5 %all-to-all-done.1.partial = bf16[4,128,1536]{2,1,0:T(8,128)(2,1)S(1)} async-done(((bf16[4,128,1536]{2,1,0:T(8,128)(2,1)}), bf16[4,128,1536]{2,1,0:T(8,128)(2,1)S(1)}, u32[]{:S(2)}, u32[]{:S(2)}) %all-to-all-start.1) | async-done | bytes 1572896 | tf_op jit(solution)/shard_map/all_to_all | solution.py:18
  89.1 16.4 %all_to_all.25 = bf16[4,128,1536]{2,1,0:T(8,128)(2,1)S(1)} all-to-all(bf16[4,128,1536]{2,1,0:T(8,128)(2,1)S(1)} %get-tuple-element.30), channel_id=1, replica_groups=mesh['pipe'=2,'expert'=64,'dp'=4] {'dp'}, dimensions={0} | all-to-all | bytes 3145728 | tf_op jit(solution)/shard_map/all_to_all | solution.py:18
  105.6 1.9 %shard_map.112 = (bf16[64,3712]{1,0:T(8,128)(2,1)S(1)}, bf16[32,3712]{1,0:T(8,128)(2,1)S(1)}, bf16[32,3712]{1,0:T(8,128)(2,1)S(1)}) custom-call(bf16[512,1536]{1,0:T(8,128)(2,1)S(1)} %bitcast.67, bf16[4,3,896,128]{3,2,1,0:T(8,128)(2,1)S(1)} %bitcast.70, bf16[128,128]{1,0:T(8,128)(2,1)S(1)} %get-tuple-element.31.score), custom_call_target="tpu_custom_call" | custom-call | flops 939524096 | bytes 6000000 | tf_op jit(solution)/shard_map/pallas_call | solution.py:182
  107.5 4.1 %shard_map.113 = bf16[4,3,896,128]{3,2,1,0:T(8,128)(2,1)} custom-call(bf16[64,7296]{1,0:T(8,128)(2,1)S(1)} %all_gather.9.own, bf16[32,7296]{1,0:T(8,128)(2,1)S(1)} %collective-permute-done.low, bf16[32,7296]{1,0:T(8,128)(2,1)S(1)} %collective-permute-done.1.high, bf16[512,1536]{1,0:T(8,128)(2,1)S(1)} %bitcast.68), custom_call_target="tpu_custom_call" | custom-call | flops 1409286144 | bytes 7000000 | tf_op jit(solution)/shard_map/pallas_call | solution.py:220
  111.6 2.4 %collective-permute-start.2 = (bf16[32,3712]{1,0:T(8,128)(2,1)S(1)}, bf16[32,3712]{1,0:T(8,128)(2,1)S(1)}, u32[]{:S(2)}, u32[]{:S(2)}) collective-permute-start(bf16[32,3712]{1,0:T(8,128)(2,1)S(1)} %get-tuple-element.35), channel_id=1, source_target_pairs={{0,4},{4,8},{8,12},{12,16},{16,20},{20,24},{24,28},{28,32},{32,36}... | collective-permute-start | bytes 712712 | tf_op jit(solution)/shard_map/ppermute | solution.py:280
  114.0 4.5 %collective-permute-start.3 = (bf16[32,3712]{1,0:T(8,128)(2,1)S(1)}, bf16[32,3712]{1,0:T(8,128)(2,1)S(1)}, u32[]{:S(2)}, u32[]{:S(2)}) collective-permute-start(bf16[32,3712]{1,0:T(8,128)(2,1)S(1)} %get-tuple-element.36), channel_id=1, source_target_pairs={{4,0},{8,4},{12,8},{16,12},{20,16},{24,20},{28,24},{32,28},{36,32}... | collective-permute-start | bytes 712712 | tf_op jit(solution)/shard_map/ppermute | solution.py:281
  118.5 1.6 collective-permute-done.2
  122.5 19.7 %all-to-all-start.3 = ((bf16[8,8,3712]{2,1,0:T(8,128)(2,1)}), bf16[8,8,3712]{2,1,0:T(8,128)(2,1)S(1)}, u32[]{:S(2)}, u32[]{:S(2)}) async-start(bf16[8,8,3712]{2,1,0:T(8,128)(2,1)} %fusion), calls=%async_computation.3 | async-start | bytes 950272 | tf_op jit(solution)/shard_map/all_to_all | solution.py:18
  142.1 18.4 %all-to-all-done.3 = bf16[8,8,3712]{2,1,0:T(8,128)(2,1)S(1)} async-done(((bf16[8,8,3712]{2,1,0:T(8,128)(2,1)}), bf16[8,8,3712]{2,1,0:T(8,128)(2,1)S(1)}, u32[]{:S(2)}, u32[]{:S(2)}) %all-to-all-start.3) | async-done | bytes 475168 | tf_op jit(solution)/shard_map/all_to_all | solution.py:18
  161.3 2.2 %reduce-scatter.2.cloned.1.call-done = bf16[1,3,896,128]{3,2,1,0:T(8,128)(2,1)} async-done(((bf16[4,3,896,128]{3,2,1,0:T(8,128)(2,1)}), bf16[1,3,896,128]{3,2,1,0:T(8,128)(2,1)}) %reduce-scatter.2.cloned.1.call-update) | async-done | bytes 688144 | tf_op jit(solution)/shard_map/reduce_scatter | solution.py:285
  164.3 13.1 %all-to-all-start.4 = ((bf16[8,8,896]{2,1,0:T(8,128)(2,1)}), bf16[8,8,896]{2,1,0:T(8,128)(2,1)S(1)}, u32[]{:S(2)}, u32[]{:S(2)}) async-start(bf16[8,8,896]{2,1,0:T(8,128)(2,1)} %bitcast.24), calls=%async_computation.5 | async-start | bytes 229376 | tf_op jit(solution)/shard_map/all_to_all | solution.py:18
  177.4 2.3 %slice_convert_fusion = (f32[1,896,128]{2,1,0:T(8,128)}, f32[1,896,128]{2,1,0:T(8,128)}, f32[1,896,128]{2,1,0:T(8,128)}) fusion(bf16[3,896,128]{2,1,0:T(8,128)(2,1)} %bitcast.72), kind=kLoop, calls=%fused_computation.4 | loop fusion | flops 344064 | bytes 2064384 | tf_op jit(solution)/shard_map/convert_element_type | solution.py:293
  179.7 2.8 %all-to-all-done.4 = bf16[8,8,896]{2,1,0:T(8,128)(2,1)S(1)} async-done(((bf16[8,8,896]{2,1,0:T(8,128)(2,1)}), bf16[8,8,896]{2,1,0:T(8,128)(2,1)S(1)}, u32[]{:S(2)}, u32[]{:S(2)}) %all-to-all-start.4) | async-done | bytes 114720 | tf_op jit(solution)/shard_map/all_to_all | solution.py:18
  (37 shorter events, 6.9 us)
Async XLA Ops:
  7.2 8.5 %copy-start.3 = (bf16[1,8,4]{1,2,0:T(4,128)(2,1)S(1)}, bf16[1,8,4]{1,2,0:T(4,128)(2,1)}, u32[]{:S(2)}) copy-start(bf16[1,8,4]{1,2,0:T(4,128)(2,1)} %param.10) | copy-start | bytes 196
  7.2 8.5 %copy-start.2 = (s32[1,8,4]{1,2,0:T(4,128)S(1)}, s32[1,8,4]{1,2,0:T(4,128)}, u32[]{:S(2)}) copy-start(s32[1,8,4]{1,2,0:T(4,128)} %param.9) | copy-start | bytes 388
  8.7 9.6 %all-to-all-start = ((bf16[4,16,896]{2,1,0:T(8,128)(2,1)}), bf16[4,16,896]{2,1,0:T(8,128)(2,1)S(1)}, u32[]{:S(2)}, u32[]{:S(2)}) async-start(bf16[4,16,896]{2,1,0:T(8,128)(2,1)} %maximum_bitcast_fusion), calls=%async_computation | async-start | bytes 229376 | tf_op jit(solution)/shard_map/all_to_all | solution.py:18
  13.5 52.5 %all-gather.3.cloned.1.call-start = ((), (), s32[]{:S(2)}) async-start(), calls=%async_computation.7 | async-start | bytes 3440640 | tf_op jit(solution)/shard_map/all_gather | solution.py:261
  54.0 11.2 %collective-permute-start = (bf16[32,7296]{1,0:T(8,128)(2,1)S(1)}, bf16[32,7296]{1,0:T(8,128)(2,1)S(1)}, u32[]{:S(2)}, u32[]{:S(2)}) collective-permute-start(bf16[32,7296]{1,0:T(8,128)(2,1)S(1)} %get-tuple-element.48), channel_id=1, source_target_pairs={{0,4},{4,8},{8,12},{12,16},{16,20},{20,24},{24,28},{28,32},{32,36}... | collective-permute-start | bytes 1400840 | tf_op jit(solution)/shard_map/ppermute | solution.py:271
  56.3 9.7 %collective-permute-start.1 = (bf16[32,7296]{1,0:T(8,128)(2,1)S(1)}, bf16[32,7296]{1,0:T(8,128)(2,1)S(1)}, u32[]{:S(2)}, u32[]{:S(2)}) collective-permute-start(bf16[32,7296]{1,0:T(8,128)(2,1)S(1)} %get-tuple-element.47), channel_id=1, source_target_pairs={{4,0},{8,4},{12,8},{16,12},{20,16},{24,20},{28,24},{32,28},{36,32}... | collective-permute-start | bytes 1400840 | tf_op jit(solution)/shard_map/ppermute | solution.py:272
  66.0 1.8 copy-start
  71.5 16.3 %all-to-all-start.1 = ((bf16[4,128,1536]{2,1,0:T(8,128)(2,1)}), bf16[4,128,1536]{2,1,0:T(8,128)(2,1)S(1)}, u32[]{:S(2)}, u32[]{:S(2)}) async-start(bf16[4,128,1536]{2,1,0:T(8,128)(2,1)} %bitcast.71), calls=%async_computation.1 | async-start | bytes 3145728 | tf_op jit(solution)/shard_map/all_to_all | solution.py:18
  75.2 88.4 %reduce-scatter.2.cloned.1.call-start = ((), (), s32[]{:S(2)}) async-start(), calls=%async_computation.6 | async-start | bytes 3440640 | tf_op jit(solution)/shard_map/reduce_scatter | solution.py:285
  89.1 16.4 %copy-start.1 = (bf16[12,896,128]{2,1,0:T(8,128)(2,1)S(1)}, bf16[12,896,128]{2,1,0:T(8,128)(2,1)}, u32[]{:S(2)}) copy-start(bf16[12,896,128]{2,1,0:T(8,128)(2,1)} %all-gather.3.cloned.1.call-done) | copy-start | bytes 8257540
  111.6 8.5 %collective-permute-start.2 = (bf16[32,3712]{1,0:T(8,128)(2,1)S(1)}, bf16[32,3712]{1,0:T(8,128)(2,1)S(1)}, u32[]{:S(2)}, u32[]{:S(2)}) collective-permute-start(bf16[32,3712]{1,0:T(8,128)(2,1)S(1)} %get-tuple-element.35), channel_id=1, source_target_pairs={{0,4},{4,8},{8,12},{12,16},{16,20},{20,24},{24,28},{28,32},{32,36}... | collective-permute-start | bytes 712712 | tf_op jit(solution)/shard_map/ppermute | solution.py:280
  114.0 7.5 %collective-permute-start.3 = (bf16[32,3712]{1,0:T(8,128)(2,1)S(1)}, bf16[32,3712]{1,0:T(8,128)(2,1)S(1)}, u32[]{:S(2)}, u32[]{:S(2)}) collective-permute-start(bf16[32,3712]{1,0:T(8,128)(2,1)S(1)} %get-tuple-element.36), channel_id=1, source_target_pairs={{4,0},{8,4},{12,8},{16,12},{20,16},{24,20},{28,24},{32,28},{36,32}... | collective-permute-start | bytes 712712 | tf_op jit(solution)/shard_map/ppermute | solution.py:281
  122.5 38.1 %all-to-all-start.3 = ((bf16[8,8,3712]{2,1,0:T(8,128)(2,1)}), bf16[8,8,3712]{2,1,0:T(8,128)(2,1)S(1)}, u32[]{:S(2)}, u32[]{:S(2)}) async-start(bf16[8,8,3712]{2,1,0:T(8,128)(2,1)} %fusion), calls=%async_computation.3 | async-start | bytes 950272 | tf_op jit(solution)/shard_map/all_to_all | solution.py:18
  164.3 18.2 %all-to-all-start.4 = ((bf16[8,8,896]{2,1,0:T(8,128)(2,1)}), bf16[8,8,896]{2,1,0:T(8,128)(2,1)S(1)}, u32[]{:S(2)}, u32[]{:S(2)}) async-start(bf16[8,8,896]{2,1,0:T(8,128)(2,1)} %bitcast.24), calls=%async_computation.5 | async-start | bytes 229376 | tf_op jit(solution)/shard_map/all_to_all | solution.py:18
Sparse Core Ops, SparseCore 0:
  16.5 49.2 all-gather.2
  111.7 51.8 reduce-scatter.1
